TPU v7x, 256 devices: a whole 4x4x8 slice. The times are simulated.
256 devices in a mesh: row: 32 (over z, x), col: 8 (over y, core).
Axes of the slice: x: 4, y: 4, z: 8, core: 2. Of those that a mesh axis runs over, the one named last changes fastest.
Arguments:
- image: bfloat16 [512, 1024, 256], P('row', 'col'), may hold values from -6 to 6
- kernel_one: bfloat16 [3, 3, 256, 256], replicated, may hold values from -0.125 to 0.125
- kernel_two: bfloat16 [3, 3, 256, 512], replicated, may hold values from -0.125 to 0.125
- cotangent: bfloat16 [256, 512, 512], P('row', 'col'), may hold values from -6 to 6
Outputs:
- image_grad: bfloat16 [512, 1024, 256], P('row', 'col')
- update_one: bfloat16 [3, 3, 256, 256], replicated
- update_two: bfloat16 [3, 3, 256, 512], replicated
All inputs are finite; a program needn't handle non-finite values.
Results may differ from a plain program's by a relative error of at most 0.006.
Values may be sent and summed in bfloat16 or wider, within the bound.
A program may use at most 128 MiB of HBM per device.

v0:
```python
import jax
import jax.numpy as jnp
from jax import lax
from jax.sharding import PartitionSpec as P


def padded(shard, sides, width):
    for axis, dim in sides:
        size, length = (lax.axis_size(axis), shard.shape[dim])
        up = [(i, (i + 1) % size) for i in range(size - 1)]
        down = [(j, i) for i, j in up]
        last = lax.slice_in_dim(shard, length - width, length, axis=dim)
        initial = lax.slice_in_dim(shard, 0, width, axis=dim)
        before = lax.ppermute(last, axis, up)
        after = lax.ppermute(initial, axis, down)
        shard = jnp.concatenate([before, shard, after], axis=dim)
    return shard


def passed_along(shard, axis, by):
    size = lax.axis_size(axis)
    pairs = [(i, i + by) for i in range(size) if 0 <= i + by < size]
    return lax.ppermute(shard, axis, pairs)


def conv_local(source, kernel, padding, dilation, layout):
    result = lax.conv_general_dilated(
        source[None],
        kernel,
        (1, 1),
        padding,
        lhs_dilation=dilation,
        dimension_numbers=("NHWC", layout, "NHWC"),
        preferred_element_type=jnp.float32,
    )
    return result[0]


def on_device(image, kernel_one, kernel_two, cotangent):
    rows_here = image.shape[0]
    cols_here = image.shape[1]
    image_pad = padded(image, (("row", 0), ("col", 1)), 1)
    pre_act = conv_local(image_pad, kernel_one, "VALID", (1, 1), "HWIO")
    activ = jax.nn.silu(pre_act).astype(jnp.bfloat16)
    left_edge = passed_along(activ[:, -1:], "col", 1)
    act_cols = jnp.concatenate([left_edge, activ], 1)
    top_edge = passed_along(act_cols[-1:], "row", 1)
    act_pad = jnp.concatenate([top_edge, act_cols], 0)
    rows_two = []
    for row_off in range(3):
        cols_two = []
        for col_off in range(3):
            patch = act_pad[
                row_off : row_off + rows_here - 1 : 2, col_off : col_off + cols_here - 1 : 2
            ]
            cols_two.append(
                jnp.einsum("ijc,ije->ce", patch, cotangent, preferred_element_type=jnp.float32)
            )
        rows_two.append(jnp.stack(cols_two))
    grad_two = jnp.stack(rows_two)
    flipped_two = kernel_two[::-1, ::-1]
    act_full = conv_local(cotangent, flipped_two, ((2, 2), (2, 2)), (2, 2), "HWOI")
    from_right = passed_along(act_full[:, :1], "col", -1)
    act_trim = act_full[:, 1:]
    act_trim = jnp.concatenate([act_trim[:, :-1], act_trim[:, -1:] + from_right], 1)
    from_below = passed_along(act_trim[:1].astype(jnp.bfloat16), "row", -1).astype(jnp.float32)
    act_grad = act_trim[1:]
    act_grad = jnp.concatenate([act_grad[:-1], act_grad[-1:] + from_below], 0)
    sig = jax.nn.sigmoid(pre_act)
    pre_grad = (act_grad * sig * (1.0 + pre_act * (1.0 - sig))).astype(jnp.bfloat16)
    rows_one = []
    for row_off in range(3):
        cols_one = []
        for col_off in range(3):
            patch = image_pad[row_off : row_off + rows_here, col_off : col_off + cols_here]
            cols_one.append(
                jnp.einsum("ijc,ijd->cd", patch, pre_grad, preferred_element_type=jnp.float32)
            )
        rows_one.append(jnp.stack(cols_one))
    grad_one = jnp.stack(rows_one)
    grad_pad = padded(pre_grad, (("row", 0), ("col", 1)), 1)
    image_grad = conv_local(grad_pad, kernel_one[::-1, ::-1], "VALID", (1, 1), "HWOI").astype(
        jnp.bfloat16
    )
    flat_one = grad_one.reshape(-1)
    flat_two = grad_two.reshape(-1)
    total_one, total_two = lax.psum((flat_one, flat_two), ("row", "col"))
    update_one = (total_one * lax.rsqrt(jnp.mean(total_one * total_one) + 1e-06)).astype(
        jnp.bfloat16
    )
    update_two = (total_two * lax.rsqrt(jnp.mean(total_two * total_two) + 1e-06)).astype(
        jnp.bfloat16
    )
    return (image_grad, update_one.reshape(kernel_one.shape), update_two.reshape(kernel_two.shape))


def solution(mesh):
    placed = (P("row", "col", None), P(), P(), P("row", "col", None))
    return jax.shard_map(
        on_device,
        mesh=mesh,
        in_specs=placed,
        out_specs=(P("row", "col", None), P(), P()),
        check_vma=False,
    )
```

profile of v0, /device:TPU:1, one launch (start us, length us, event | category | flops | bytes accessed | tf_op | source)
XLA Modules:
  0.0 439.6 jit_solution(7343728317577428346)
XLA Ops:
  10.7 2.6 copy.37
  13.3 4.1 reshape.29
  20.8 5.1 %collective-permute-start = (f32[17,1,256]{2,1,0:T(1,128)S(1)}, f32[17,1,256]{2,1,0:T(1,128)S(1)}, u32[]{:S(2)}, u32[]{:S(2)}) collective-permute-start(f32[17,1,256]{2,1,0:T(1,128)S(1)} %slice.157), channel_id=1, source_target_pairs={{1,0},{2,1},{3,2},{4,3},{5,4},{6,5},{7,6},{9,8},{10,9},{11,10},{12... | collective-permute-start | bytes 52232 | tf_op jit(solution)/shard_map/ppermute | solution.py:23
  37.7 3.7 collective-permute-start.4
  50.0 4.4 maximum_bitcast_fusion
  54.4 3.9 copy.64
  58.2 2.5 pad.2.clone
  60.7 3.2 reshape.32
  65.9 3.0 convolution_select_fusion.1
  69.0 3.6 maximum_maximum_fusion
  76.8 2.7 slice.143
  79.5 2.7 slice.142
  82.1 2.7 slice.146
  84.9 2.7 slice.145
  93.1 3.8 collective-permute-start.10
  102.7 2.6 copy.65
  105.8 2.7 slice.141
  109.0 4.5 %collective-permute-start.11 = (bf16[1,129,256]{2,1,0:T(8,128)(2,1)S(1)}, bf16[1,129,256]{2,1,0:T(8,128)(2,1)S(1)}, u32[]{:S(2)}, u32[]{:S(2)}) collective-permute-start(bf16[1,129,256]{2,1,0:T(8,128)(2,1)S(1)} %fusion.42), channel_id=1, source_target_pairs={{0,8},{8,16},{16,24},{24,32},{32,40},{40,48},{48,56},{56,64},{64,7... | collective-permute-start | bytes 198152 | tf_op jit(solution)/shard_map/ppermute | solution.py:23
  117.9 2.7 slice.140
  120.6 2.7 slice.139
  130.1 3.4 copy.66
  133.5 3.6 collective-permute-start.6
  138.4 4.7 %collective-permute-done.7 = bf16[1,128,256]{2,1,0:T(8,128)(2,1)S(1)} collective-permute-done((bf16[1,128,256]{2,1,0:T(8,128)(2,1)S(1)}, bf16[1,128,256]{2,1,0:T(8,128)(2,1)S(1)}, u32[]{:S(2)}, u32[]{:S(2)}) %collective-permute-start.7) | collective-permute-done | bytes 65568 | tf_op jit(solution)/shard_map/ppermute | solution.py:15
  143.1 3.8 collective-permute-start.8
  149.2 2.9 collective-permute-done.9
  154.0 2.3 reshape.39
  157.6 2.8 select_convert_fusion
  162.0 254.4 %all-reduce.3.cloned.1.call-done = (f32[589824]{0:T(1024)}, f32[1179648]{0:T(1024)}) async-done(((f32[589824]{0:T(1024)}, f32[1179648]{0:T(1024)}), (f32[589824]{0:T(1024)}, f32[1179648]{0:T(1024)})) %all-reduce.3.cloned.1.call-update) | async-done | bytes 7077904 | tf_op jit(solution)/shard_map/psum | solution.py:87
  416.4 3.6 multiply_reduce_fusion
  420.7 2.5 multiply_convert_fusion
  423.2 2.7 reshape.22
  425.9 2.9 multiply_reduce_fusion.1
  (140 shorter events, 68.0 us)
Async XLA Ops:
  7.2 409.2 %all-reduce.3.cloned.1.call-start = ((), (), s32[]{:S(2)}) async-start(), calls=%async_computation | async-start | bytes 14155776 | tf_op jit(solution)/shard_map/psum | solution.py:87
  17.4 8.5 %copy-start.9 = (bf16[16,128,256]{2,1,0:T(8,128)(2,1)S(1)}, bf16[16,128,256]{2,1,0:T(8,128)(2,1)}, u32[]{:S(2)}) copy-start(bf16[16,128,256]{2,1,0:T(8,128)(2,1)} %param.4) | copy-start | bytes 3145732
  20.8 10.5 %collective-permute-start = (f32[17,1,256]{2,1,0:T(1,128)S(1)}, f32[17,1,256]{2,1,0:T(1,128)S(1)}, u32[]{:S(2)}, u32[]{:S(2)}) collective-permute-start(f32[17,1,256]{2,1,0:T(1,128)S(1)} %slice.157), channel_id=1, source_target_pairs={{1,0},{2,1},{3,2},{4,3},{5,4},{6,5},{7,6},{9,8},{10,9},{11,10},{12... | collective-permute-start | bytes 52232 | tf_op jit(solution)/shard_map/ppermute | solution.py:23
  26.6 7.1 %collective-permute-start.2 = (bf16[1,128,256]{1,2,0:T(8,128)(2,1)S(1)}, bf16[1,128,256]{1,2,0:T(8,128)(2,1)S(1)}, u32[]{:S(2)}, u32[]{:S(2)}) collective-permute-start(bf16[1,128,256]{1,2,0:T(8,128)(2,1)S(1)} %get-tuple-element.21), channel_id=1, source_target_pairs={{0,8},{8,16},{16,24},{24,32},{32,40},{40,48},{48,56},{56,64},{64,7... | collective-permute-start | bytes 196616 | tf_op jit(solution)/shard_map/ppermute | solution.py:14
  28.0 5.9 %collective-permute-start.3 = (bf16[1,128,256]{1,2,0:T(8,128)(2,1)S(1)}, bf16[1,128,256]{1,2,0:T(8,128)(2,1)S(1)}, u32[]{:S(2)}, u32[]{:S(2)}) collective-permute-start(bf16[1,128,256]{1,2,0:T(8,128)(2,1)S(1)} %get-tuple-element.22), channel_id=1, source_target_pairs={{8,0},{16,8},{24,16},{32,24},{40,32},{48,40},{56,48},{64,56},{72,6... | collective-permute-start | bytes 196616 | tf_op jit(solution)/shard_map/ppermute | solution.py:15
  37.7 9.3 %collective-permute-start.4 = (bf16[18,1,256]{2,0,1:T(8,128)(2,1)S(1)}, bf16[18,1,256]{2,0,1:T(8,128)(2,1)S(1)}, u32[]{:S(2)}, u32[]{:S(2)}) collective-permute-start(bf16[18,1,256]{2,0,1:T(8,128)(2,1)S(1)} %copy.41), channel_id=1, source_target_pairs={{0,1},{1,2},{2,3},{3,4},{4,5},{5,6},{6,7},{8,9},{9,10},{10,11},{11... | collective-permute-start | bytes 27656 | tf_op jit(solution)/shard_map/ppermute | solution.py:14
  43.2 5.4 %collective-permute-start.5 = (bf16[18,1,256]{2,0,1:T(8,128)(2,1)S(1)}, bf16[18,1,256]{2,0,1:T(8,128)(2,1)S(1)}, u32[]{:S(2)}, u32[]{:S(2)}) collective-permute-start(bf16[18,1,256]{2,0,1:T(8,128)(2,1)S(1)} %copy.42), channel_id=1, source_target_pairs={{1,0},{2,1},{3,2},{4,3},{5,4},{6,5},{7,6},{9,8},{10,9},{11,10},{12... | collective-permute-start | bytes 27656 | tf_op jit(solution)/shard_map/ppermute | solution.py:15
  45.8 27.7 %collective-permute-start.1 = (bf16[1,128,256]{2,1,0:T(8,128)(2,1)}, bf16[1,128,256]{2,1,0:T(8,128)(2,1)S(1)}, u32[]{:S(2)}, u32[]{:S(2)}) collective-permute-start(bf16[1,128,256]{2,1,0:T(8,128)(2,1)} %fusion.41), channel_id=1, source_target_pairs={{8,0},{16,8},{24,16},{32,24},{40,32},{48,40},{56,48},{64,56},{72,6... | collective-permute-start | bytes 196616 | tf_op jit(solution)/shard_map/ppermute | solution.py:23
  64.0 1.9 copy-start.26
  65.9 3.0 copy-start.2
  65.9 3.0 copy-start.3
  87.6 2.0 copy-start.8
  87.6 2.7 copy-start.7
  92.1 4.8 %copy-start.14 = (bf16[8,64,512]{2,1,0:T(8,128)(2,1)S(1)}, bf16[8,64,512]{2,1,0:T(8,128)(2,1)}, u32[]{:S(2)}) copy-start(bf16[8,64,512]{2,1,0:T(8,128)(2,1)} %param.7) | copy-start | bytes 1572868
  92.1 4.8 %copy-start.21 = (bf16[8,64,256]{2,1,0:T(8,128)(2,1)S(1)}, bf16[8,64,256]{2,1,0:T(8,128)(2,1)}, u32[]{:S(2)}) copy-start(bf16[8,64,256]{2,1,0:T(8,128)(2,1)} %slice.143) | copy-start | bytes 786436
  92.5 5.5 %copy-start.20 = (bf16[8,64,256]{2,1,0:T(8,128)(2,1)S(1)}, bf16[8,64,256]{2,1,0:T(8,128)(2,1)}, u32[]{:S(2)}) copy-start(bf16[8,64,256]{2,1,0:T(8,128)(2,1)} %slice.142) | copy-start | bytes 786436
  93.1 6.1 %copy-start.19 = (bf16[8,64,256]{2,1,0:T(8,128)(2,1)S(1)}, bf16[8,64,256]{2,1,0:T(8,128)(2,1)}, u32[]{:S(2)}) copy-start(bf16[8,64,256]{2,1,0:T(8,128)(2,1)} %slice.146) | copy-start | bytes 786436
  93.1 7.2 %copy-start.18 = (bf16[8,64,256]{2,1,0:T(8,128)(2,1)S(1)}, bf16[8,64,256]{2,1,0:T(8,128)(2,1)}, u32[]{:S(2)}) copy-start(bf16[8,64,256]{2,1,0:T(8,128)(2,1)} %slice.145) | copy-start | bytes 786436
  93.1 12.2 %collective-permute-start.10 = (bf16[16,1,256]{2,1,0:T(2,128)(2,1)S(1)}, bf16[16,1,256]{2,1,0:T(2,128)(2,1)S(1)}, u32[]{:S(2)}, u32[]{:S(2)}) collective-permute-start(bf16[16,1,256]{2,1,0:T(2,128)(2,1)S(1)} %slice.178), channel_id=1, source_target_pairs={{0,1},{1,2},{2,3},{3,4},{4,5},{5,6},{6,7},{8,9},{9,10},{10,11},{11... | collective-permute-start | bytes 24584 | tf_op jit(solution)/shard_map/ppermute | solution.py:23
  105.3 10.5 %copy-start.22 = (bf16[16,1,256]{2,1,0:T(2,128)(2,1)}, bf16[16,1,256]{2,1,0:T(2,128)(2,1)S(1)}, u32[]{:S(2)}) copy-start(bf16[16,1,256]{2,1,0:T(2,128)(2,1)S(1)} %collective-permute-done.10) | copy-start | bytes 24580
  108.9 6.9 %copy-start.15 = (bf16[8,64,512]{2,1,0:T(8,128)(2,1)S(1)}, bf16[8,64,512]{2,1,0:T(8,128)(2,1)}, u32[]{:S(2)}) copy-start(bf16[8,64,512]{2,1,0:T(8,128)(2,1)} %param.7) | copy-start | bytes 1572868
  108.9 7.2 %copy-start.16 = (f32[1,256,512]{2,1,0:T(8,128)S(1)}, f32[1,256,512]{2,1,0:T(8,128)}, u32[]{:S(2)}) copy-start(f32[1,256,512]{2,1,0:T(8,128)} %convolution_bitcast_fusion) | copy-start | bytes 1572868
  108.9 7.2 %copy-start.17 = (f32[1,256,512]{2,1,0:T(8,128)S(1)}, f32[1,256,512]{2,1,0:T(8,128)}, u32[]{:S(2)}) copy-start(f32[1,256,512]{2,1,0:T(8,128)} %convolution_bitcast_fusion.1) | copy-start | bytes 1572868
  109.0 8.5 %collective-permute-start.11 = (bf16[1,129,256]{2,1,0:T(8,128)(2,1)S(1)}, bf16[1,129,256]{2,1,0:T(8,128)(2,1)S(1)}, u32[]{:S(2)}, u32[]{:S(2)}) collective-permute-start(bf16[1,129,256]{2,1,0:T(8,128)(2,1)S(1)} %fusion.42), channel_id=1, source_target_pairs={{0,8},{8,16},{16,24},{24,32},{32,40},{40,48},{48,56},{56,64},{64,7... | collective-permute-start | bytes 198152 | tf_op jit(solution)/shard_map/ppermute | solution.py:23
  123.7 4.4 %copy-start.11 = (f32[1,256,512]{2,1,0:T(8,128)S(1)}, f32[1,256,512]{2,1,0:T(8,128)}, u32[]{:S(2)}) copy-start(f32[1,256,512]{2,1,0:T(8,128)} %convolution_bitcast_fusion.3) | copy-start | bytes 1572868
  123.7 4.4 %copy-start.12 = (f32[1,256,512]{2,1,0:T(8,128)S(1)}, f32[1,256,512]{2,1,0:T(8,128)}, u32[]{:S(2)}) copy-start(f32[1,256,512]{2,1,0:T(8,128)} %convolution_bitcast_fusion.4) | copy-start | bytes 1572868
  123.7 4.4 %copy-start.13 = (f32[1,256,512]{2,1,0:T(8,128)S(1)}, f32[1,256,512]{2,1,0:T(8,128)}, u32[]{:S(2)}) copy-start(f32[1,256,512]{2,1,0:T(8,128)} %convolution_bitcast_fusion.5) | copy-start | bytes 1572868
  133.5 5.0 %collective-permute-start.6 = (bf16[1,128,256]{2,1,0:T(8,128)(2,1)S(1)}, bf16[1,128,256]{2,1,0:T(8,128)(2,1)S(1)}, u32[]{:S(2)}, u32[]{:S(2)}) collective-permute-start(bf16[1,128,256]{2,1,0:T(8,128)(2,1)S(1)} %get-tuple-element.19), channel_id=1, source_target_pairs={{0,8},{8,16},{16,24},{24,32},{32,40},{40,48},{48,56},{56,64},{64,7... | collective-permute-start | bytes 196616 | tf_op jit(solution)/shard_map/ppermute | solution.py:14
  137.1 6.0 %collective-permute-start.7 = (bf16[1,128,256]{2,1,0:T(8,128)(2,1)S(1)}, bf16[1,128,256]{2,1,0:T(8,128)(2,1)S(1)}, u32[]{:S(2)}, u32[]{:S(2)}) collective-permute-start(bf16[1,128,256]{2,1,0:T(8,128)(2,1)S(1)} %get-tuple-element.20), channel_id=1, source_target_pairs={{8,0},{16,8},{24,16},{32,24},{40,32},{48,40},{56,48},{64,56},{72,6... | collective-permute-start | bytes 196616 | tf_op jit(solution)/shard_map/ppermute | solution.py:15
  143.1 6.0 %collective-permute-start.8 = (bf16[18,1,256]{2,1,0:T(2,128)(2,1)S(1)}, bf16[18,1,256]{2,1,0:T(2,128)(2,1)S(1)}, u32[]{:S(2)}, u32[]{:S(2)}) collective-permute-start(bf16[18,1,256]{2,1,0:T(2,128)(2,1)S(1)} %get-tuple-element.15), channel_id=1, source_target_pairs={{0,1},{1,2},{2,3},{3,4},{4,5},{5,6},{6,7},{8,9},{9,10},{10,11},{11... | collective-permute-start | bytes 27656 | tf_op jit(solution)/shard_map/ppermute | solution.py:14
  147.0 5.1 %collective-permute-start.9 = (bf16[18,1,256]{2,1,0:T(2,128)(2,1)S(1)}, bf16[18,1,256]{2,1,0:T(2,128)(2,1)S(1)}, u32[]{:S(2)}, u32[]{:S(2)}) collective-permute-start(bf16[18,1,256]{2,1,0:T(2,128)(2,1)S(1)} %get-tuple-element.16), channel_id=1, source_target_pairs={{1,0},{2,1},{3,2},{4,3},{5,4},{6,5},{7,6},{9,8},{10,9},{11,10},{12... | collective-permute-start | bytes 27656 | tf_op jit(solution)/shard_map/ppermute | solution.py:15
  429.5 3.2 copy-start.1
  (9 other events, 13.8 us)
Sparse Core Ops, SparseCore 0:
  133.6 282.8 all-reduce.2
where the time goes:
time: 441 us; the launch traced here: 440 us
  waiting for transfers between devices  262 us (59%)
  local copies, waits for them, and re-layouts  74.6 us (17%)
  starting transfers between devices  34 us (8%)
  other arithmetic  28 us (6%)
  matrix products  24.6 us (6%)
  between operations  16.2 us (4%)
    psum x1, waiting for transfers between devices, on_device(): total_one, total_two = lax.psum((flat_one, flat_two), ('row', 'col'))  254 us
    slice x9, local copies, waits for them, and re-layouts, on_device(): act_pad[row_off:row_off + rows_here - 1:2, col_off:col_off + cols_here -...  19.8 us
    unnamed x62, local copies, waits for them, and re-layouts  19 us
    conv_general_dilated x12, local copies, waits for them, and re-layouts, conv_local(): lax.conv_general_dilated(source[None], kernel, (1, 1), padding, lhs_dilat...  15.6 us
    ppermute x4, starting transfers between devices, passed_along(): return lax.ppermute(shard, axis, pairs)  14.7 us
    ppermute x4, starting transfers between devices, padded(): before = lax.ppermute(last, axis, up)  12.5 us
    dot_general x9, matrix products, on_device(): jnp.einsum('ijc,ije->ce', patch, cotangent, preferred_element_type=jnp.fl...  11.4 us
  transfers between devices with their start and end apart: 13, of which 4 were waited for; matrix products, arithmetic and copies ran while one was open for 13% of the time, Pallas kernels for 0%

commit v1 on v0

v1 whole, which is shorter than its diff:
```python
import functools

import jax
import jax.numpy as jnp
from jax import lax
from jax.experimental import pallas as pl
from jax.experimental.pallas import tpu as pltpu
from jax.sharding import PartitionSpec as P

MESH = pl.DeviceIdType.MESH
bf16, f32 = jnp.bfloat16, jnp.float32
ROWS, COLS = 32, 8
NX, NY, NZ = 4, 4, 8
JOBS = ((0, 0, 2304, "yx"), (1, 0, 2304, "xy"), (2, 0, 1280, "yx"), (2, 1280, 1024, "xy"))


def dot(a, b):
    return jnp.dot(a, b, preferred_element_type=f32)


def dot_nt(a, b):
    return lax.dot_general(a, b, (((1,), (1,)), ((), ())), preferred_element_type=f32)


def dot_tn(a, b):
    return lax.dot_general(a, b, (((0,), (0,)), ((), ())), preferred_element_type=f32)


def total_of(terms):
    return functools.reduce(lambda u, v: u + v, terms)


def kernel(
    image_hbm, k1_hbm, k2_hbm, cot_hbm,
    image_grad, two, one,
    image, k1, k2, cot, F, X, V, A, D, C, Cs,
    edge32, edges, hrow, hcol, cedge, crow, ccol, pedges, prow, pcol, left, right,
    T2, R2, T1, R1, S, P1, Q1, P2, Zs, Zr, G,
    load_sem,
    img_s, img_r, cot_s, cot_r, pg_s, pg_r, c2_s, c2_r, c1_s, c1_r,
    a1_s, a1_r, a2_s, a2_r, az_s, az_r, gz_s, gz_r, g2_s, g2_r, g1_s, g1_r, gc_s, gc_r,
):
    row, col = lax.axis_index("row"), lax.axis_index("col")
    z, x, y, core = row // NX, row % NX, col // 2, col % 2
    other = 1 - core

    def at_row(d):
        return (row + d + ROWS) % ROWS

    def at_col(d):
        return (col + d + COLS) % COLS

    def at_x(k):
        return (z * NX + (x + k) % NX, col)

    def at_y(k):
        return (row, ((y + k) % NY) * 2 + core)

    def at_z(k):
        return (((z + k) % NZ) * NX + x, col)

    sibling = (row, y * 2 + other)
    around = [(at_row(u), at_col(v)) for u in (-1, 0, 1) for v in (-1, 0, 1) if (u, v) != (0, 0)]
    pending = []

    def send(src, dst, send_sem, recv_sem, to):
        copy = pltpu.make_async_remote_copy(
            src_ref=src, dst_ref=dst, send_sem=send_sem, recv_sem=recv_sem, device_id=to, device_id_type=MESH
        )
        copy.start()
        pending.append(copy)
        return copy

    loads = []
    for n, (src, dst) in enumerate(((image_hbm, image), (cot_hbm, cot), (k1_hbm, k1), (k2_hbm, k2))):
        copy = pltpu.make_async_copy(src, dst, load_sem.at[n])
        copy.start()
        loads.append(copy)

    barrier = pltpu.get_barrier_semaphore()
    greeted = around + [sibling] + [at_y(k) for k in (1, 2, 3)] + [at_x(k) for k in (1, 2, 3)] + [at_z(k) for k in range(1, NZ)]
    for to in greeted:
        pl.semaphore_signal(barrier, inc=1, device_id=to, device_id_type=MESH)

    def spread(slot, values):
        v = values.astype(f32)
        F[slot, 0] = v[:, :128]
        F[slot, 1] = v[:, 128:]

    loads[0].wait()

    @pl.loop(0, 16)
    def _(p):
        spread(p, image[p])

    for p in range(16):
        for h in range(2):
            edge32[0, p : p + 1, 128 * h : 128 * h + 128] = F[p, h, 0:1, :]
            edge32[1, p : p + 1, 128 * h : 128 * h + 128] = F[p, h, 127:128, :]
    edges[...] = edge32[...].astype(bf16)
    loads[1].wait()
    edge2 = [cot[i, 0:16, :].astype(f32)[0:1] for i in range(8)]
    cedge[...] = jnp.concatenate(edge2 + [jnp.zeros((8, 512), f32)], axis=0).astype(bf16)

    pl.semaphore_wait(barrier, len(greeted))

    def send_halos(first, last, ends, rows_to, cols_to, send_sem, recv_sem):
        sent = [
            send(first, rows_to.at[1], send_sem.at[0], recv_sem.at[0], (at_row(-1), col)),
            send(last, rows_to.at[0], send_sem.at[1], recv_sem.at[1], (at_row(1), col)),
        ]
        n = 2
        for side, v in ((1, -1), (0, 1)):
            for place, u in ((0, 1), (1, 0), (2, -1)):
                to = (at_row(u) if u else row, at_col(v))
                sent.append(send(ends.at[1 - side], cols_to.at[side, place], send_sem.at[n], recv_sem.at[n], to))
                n += 1
        return sent

    halo = send_halos(image.at[0], image.at[15], edges, hrow, hcol, img_s, img_r)
    cot_halo = [
        send(cot.at[0], crow, cot_s.at[0], cot_r.at[0], (at_row(-1), col)),
        send(cedge, ccol.at[0], cot_s.at[1], cot_r.at[1], (row, at_col(-1))),
        send(cedge, ccol.at[1], cot_s.at[2], cot_r.at[2], (at_row(-1), at_col(-1))),
    ]

    def sides_of(cols_to):
        for side, ref, none in ((0, left, col == 0), (1, right, col == COLS - 1)):
            above = jnp.where((row == 0) | none, 0.0, cols_to[side, 0].astype(f32)[15:16])
            mid = jnp.where(none, 0.0, cols_to[side, 1].astype(f32))
            below = jnp.where((row == ROWS - 1) | none, 0.0, cols_to[side, 2].astype(f32)[0:1])
            ref[0:1] = above
            ref[1:17] = mid
            ref[17:18] = below

    first_at = lax.broadcasted_iota(jnp.int32, (64, 256), 0) == 0
    last_at = lax.broadcasted_iota(jnp.int32, (64, 256), 0) == 63

    def shifted(ref, r, even, odd, centre):
        before = jnp.where(first_at, left[pl.ds(r, 1)], pltpu.roll(odd, 1, 0)).astype(bf16)
        after = jnp.where(last_at, right[pl.ds(r, 1)], pltpu.roll(even, 63, 0)).astype(bf16)
        e, o = even.astype(bf16), odd.astype(bf16)
        ref[r, 0:64, 0:256] = before
        ref[r, 64:128, 0:256] = e
        if centre:
            ref[r, 0:64, 256:512] = e
            ref[r, 64:128, 256:512] = o
        ref[r, 0:64, 512:768] = o
        ref[r, 64:128, 512:768] = after

    def columns_of(slot, odd):
        return jnp.concatenate([F[slot, h, pl.ds(odd, 64, stride=2), :] for h in (0, 1)], axis=1)

    for copy in halo:
        copy.wait_recv()
    sides_of(hcol)
    spread(16, jnp.where(row == 0, 0.0, hrow[0].astype(f32)))
    spread(17, jnp.where(row == ROWS - 1, 0.0, hrow[1].astype(f32)))

    @pl.loop(0, 16)
    def _(p):
        shifted(X, p + 1, columns_of(p, 0), columns_of(p, 1), True)

    shifted(X, 0, columns_of(16, 0), columns_of(16, 1), True)
    shifted(X, 17, columns_of(17, 0), columns_of(17, 1), True)

    loads[2].wait()

    @pl.loop(0, 4)
    def _(g):
        acc = total_of(
            [dot(X[pl.ds(4 * g + a, 4)].reshape(512, 768), k1[768 * a : 768 * a + 768, :]) for a in range(3)]
        )
        s = jax.nn.sigmoid(acc)
        act = (acc * s).astype(bf16).reshape(4, 128, 256)
        D[pl.ds(4 * g, 4)] = (s * (1.0 + acc * (1.0 - s))).reshape(4, 128, 256)
        for u in range(4):
            for c in range(2):
                A[u % 2, c, 2 * g + u // 2] = act[u, 64 * c : 64 * c + 64]

    for copy in cot_halo:
        copy.wait_recv()
    no_right, no_below = col == COLS - 1, row == ROWS - 1
    end_at = lax.broadcasted_iota(jnp.int32, (64, 512), 0) == 63
    for i in range(9):
        if i < 8:
            here = cot[i].astype(f32)
            beside = ccol[0].astype(f32)[i : i + 1]
        else:
            here = jnp.where(no_below, 0.0, crow[...].astype(f32))
            beside = jnp.where(no_below, 0.0, ccol[1].astype(f32)[0:1])
        beside = jnp.where(no_right, 0.0, beside)
        C[i] = here.astype(bf16)
        Cs[i] = jnp.where(end_at, beside, pltpu.roll(here, 63, 0)).astype(bf16)

    core_two = []
    for a in range(3):
        first = 1 if a == 0 else 0
        for b in range(3):
            lhs = A[(a + 1) % 2, (b + 1) % 2].reshape(512, 256)
            for h in range(2):
                rhs = (Cs if b == 0 else C)[first : first + 8, :, 256 * h : 256 * h + 256].reshape(512, 256)
                T2[h, (3 * a + b) * 256 : (3 * a + b) * 256 + 256, :] = dot_tn(lhs, rhs).astype(bf16)
        span = pl.ds(768 * a, 768)
        core_two.append(send(T2.at[other, span], R2.at[span], c2_s.at[a], c2_r.at[a], sibling))

    loads[3].wait()

    def tap(a, b):
        return k2[(3 * a + b) * 256 : (3 * a + b) * 256 + 256, :]

    @pl.loop(0, 2)
    def _(g):
        for rp in range(2):
            for cp in range(2):
                terms = []
                for a, d in ((1, 0),) if rp == 0 else ((2, 0), (0, 1)):
                    for b, ref in ((1, C),) if cp == 0 else ((2, C), (0, Cs)):
                        terms.append(dot_nt(ref[pl.ds(4 * g + d, 4)].reshape(256, 512), tap(a, b)))
                acc = total_of(terms).reshape(4, 64, 256)
                for u in range(4):
                    p = 2 * (4 * g + u) + rp
                    V[p + 1, 64 * cp : 64 * cp + 64, 256:512] = (acc[u] * D[p, 64 * cp : 64 * cp + 64]).astype(bf16)

    for p in range(16):
        edge32[0, p : p + 1] = V[p + 1, 0:16, 256:512].astype(f32)[0:1]
        edge32[1, p : p + 1] = V[p + 1, 112:128, 256:512].astype(f32)[15:16]
    pedges[...] = edge32[...].astype(bf16)
    pg_halo = send_halos(V.at[1, :, 256:512], V.at[16, :, 256:512], pedges, prow, pcol, pg_s, pg_r)

    def axis_of(name):
        return (y, at_y, NY) if name == "y" else (x, at_x, NX)

    def places(job):
        j, base, rows, order = job
        o1, o2 = (320, 80) if base else (0, 0)
        return j, base, rows // 4, rows // 16, o1, o2, axis_of(order[0]), axis_of(order[1])

    def spans(job):
        j, base, n1, n2, o1, o2, (i1, _, _), (i2, _, _) = places(job)
        return base + n1 * i1, base + n1 * i1 + n2 * i2

    def al(v):
        return pl.multiple_of(v, 16)

    def stage1(n):
        j, base, n1, n2, o1, o2, (i1, to, _), _ = places(JOBS[n])
        return [
            send(
                S.at[j, pl.ds(al(base + n1 * ((i1 + k) % 4)), n1)], P1.at[j, k - 1, pl.ds(o1, n1)],
                a1_s.at[n, k - 1], a1_r.at[n, k - 1], to(k),
            )
            for k in (1, 2, 3)
        ]

    def stage2(n, arrived):
        j, base, n1, n2, o1, o2, (i1, _, _), (i2, to, _) = places(JOBS[n])
        for copy in arrived:
            copy.wait_recv()
        own = S[j, pl.ds(al(base + n1 * i1), n1)].astype(f32)
        Q1[j, o1 : o1 + n1] = total_of([own] + [P1[j, k, o1 : o1 + n1].astype(f32) for k in range(3)]).astype(bf16)
        return [
            send(
                Q1.at[j, pl.ds(al(o1 + n2 * ((i2 + k) % 4)), n2)], P2.at[j, k - 1, pl.ds(o2, n2)],
                a2_s.at[n, k - 1], a2_r.at[n, k - 1], to(k),
            )
            for k in (1, 2, 3)
        ]

    def stage_z(j, numbers, arrived):
        for copy in arrived:
            copy.wait_recv()
        for n in numbers:
            _, base, n1, n2, o1, o2, _, (i2, _, _) = places(JOBS[n])
            own = Q1[j, pl.ds(al(o1 + n2 * i2), n2)].astype(f32)
            summed = total_of([own] + [P2[j, k, o2 : o2 + n2].astype(f32) for k in range(3)]).astype(bf16)
            for u in range(n2 // 16):
                unit = o2 // 16 + u
                block = summed[16 * u : 16 * u + 16]
                if unit < NZ:
                    Zs[j, unit, 0:16] = block
                else:
                    for k in range(NZ):
                        Zs[j, k, 16:32] = block
        Zr[j, z] = Zs[j, z]
        return [send(Zs.at[j, (z + k) % NZ], Zr.at[j, z], az_s.at[j, k - 1], az_r.at[j, k - 1], at_z(k)) for k in range(1, NZ)]

    def unit_at(j, unit):
        if j < 2:
            return spans(JOBS[j])[1] + 16 * unit
        second = unit // 5
        return (1 - second) * (spans(JOBS[2])[1] + 16 * unit) + second * (spans(JOBS[3])[1] + 16 * (unit - 5))

    def gather_z(j, arrived):
        for copy in arrived:
            copy.wait_recv()
        summed = total_of([Zr[j, k].astype(f32) for k in range(NZ)]).astype(bf16)
        mine = pl.ds(al(unit_at(j, z)), 16)
        G[j, core, mine] = summed[0:16]
        G[j, core, pl.ds(al(unit_at(j, NZ)), 16)] = summed[16:32]
        here = G.at[j, core, mine]
        return [send(here, here, gz_s.at[j, k - 1], gz_r.at[j, k - 1], at_z(k)) for k in range(1, NZ)]

    def gather2(n, arrived):
        j, base, n1, n2, o1, o2, _, (i2, to, _) = places(JOBS[n])
        for copy in arrived:
            copy.wait_recv()
        here = G.at[j, core, pl.ds(al(spans(JOBS[n])[1]), n2)]
        return [send(here, here, g2_s.at[n, k - 1], g2_r.at[n, k - 1], to(k)) for k in (1, 2, 3)]

    def to_sibling(n, k):
        j, base, n1, n2, o1, o2, (i1, _, _), _ = places(JOBS[n])
        here = G.at[j, core, pl.ds(al(base + n1 * ((i1 - k + 4) % 4)), n1)]
        return send(here, here, gc_s.at[n, k], gc_r.at[n, k], sibling)

    def gather1(n, arrived):
        j, base, n1, n2, o1, o2, (i1, to, _), _ = places(JOBS[n])
        for copy in arrived:
            copy.wait_recv()
        here = G.at[j, core, pl.ds(al(spans(JOBS[n])[0]), n1)]
        sent = [send(here, here, g1_s.at[n, k - 1], g1_r.at[n, k - 1], to(k)) for k in (1, 2, 3)]
        return sent, [to_sibling(n, 0)]

    def forward(n, arrived):
        sent, across = arrived
        for k in (1, 2, 3):
            sent[k - 1].wait_recv()
            across.append(to_sibling(n, k))
        return across

    for copy in core_two:
        copy.wait_recv()

    @pl.loop(0, 9)
    def _(g):
        span = pl.ds(pl.multiple_of(256 * g, 256), 256)
        both = T2[core, span].astype(f32) + R2[span].astype(f32)
        S[0, span] = both[:, :128].astype(bf16)
        S[1, span] = both[:, 128:].astype(bf16)

    two_1 = [stage1(0), stage1(1)]

    core_one = []
    for a in range(3):
        for b in range(3):
            lhs = X[a : a + 16, :, 256 * b : 256 * b + 256].reshape(2048, 256)
            out = dot_tn(lhs, V[1:17, :, 256:512].reshape(2048, 256)).astype(bf16)
            for h in range(2):
                T1[h, (3 * a + b) * 256 : (3 * a + b) * 256 + 256, :] = out[:, 128 * h : 128 * h + 128]
        span = pl.ds(768 * a, 768)
        core_one.append(send(T1.at[other, span], R1.at[span], c1_s.at[a], c1_r.at[a], sibling))

    for copy in pg_halo:
        copy.wait_recv()
    sides_of(pcol)

    @pl.loop(0, 16)
    def _(p):
        shifted(V, p + 1, V[p + 1, 0:64, 256:512].astype(f32), V[p + 1, 64:128, 256:512].astype(f32), False)

    for place, r, none in ((0, 0, row == 0), (1, 17, row == ROWS - 1)):
        values = jnp.where(none, 0.0, prow[place].astype(f32))
        shifted(V, r, values[0:64], values[64:128], True)

    for copy in core_one:
        copy.wait_recv()

    @pl.loop(0, 9)
    def _(g):
        span = pl.ds(pl.multiple_of(256 * g, 256), 256)
        S[2, span] = (T1[core, span].astype(f32) + R1[span].astype(f32)).astype(bf16)

    one_1 = [stage1(2), stage1(3)]

    def image_rows(g):
        terms = []
        for a in range(3):
            for b in range(3):
                m = 3 * (2 - a) + (2 - b)
                lhs = V[pl.ds(4 * g + a, 4), :, 256 * b : 256 * b + 256].reshape(512, 256)
                terms.append(dot_nt(lhs, k1[256 * m : 256 * m + 256, :]))
        acc = total_of(terms).reshape(4, 128, 256)
        for u in range(4):
            p = 4 * g + u
            for h in range(2):
                F[p, h, pl.ds(0, 64, stride=2), :] = acc[u, 0:64, 128 * h : 128 * h + 128]
                F[p, h, pl.ds(1, 64, stride=2), :] = acc[u, 64:128, 128 * h : 128 * h + 128]
            image_grad[p] = jnp.concatenate([F[p, 0], F[p, 1]], axis=1).astype(bf16)

    pl.loop(0, 2)(image_rows)
    two_2 = [stage2(0, two_1[0]), stage2(1, two_1[1])]
    pl.loop(2, 4)(image_rows)
    two_z = [stage_z(0, (0,), two_2[0]), stage_z(1, (1,), two_2[1])]
    one_2 = [stage2(2, one_1[0]), stage2(3, one_1[1])]
    two_gz = [gather_z(0, two_z[0]), gather_z(1, two_z[1])]
    one_z = stage_z(2, (2, 3), one_2[0] + one_2[1])
    two_g2 = [gather2(0, two_gz[0]), gather2(1, two_gz[1])]
    one_gz = gather_z(2, one_z)
    two_g1 = [gather1(0, two_g2[0]), gather1(1, two_g2[1])]
    one_g2 = [gather2(2, one_gz), gather2(3, [])]
    one_g1 = [gather1(2, one_g2[0]), gather1(3, one_g2[1])]
    two_c = [forward(0, two_g1[0]), forward(1, two_g1[1])]
    one_c = [forward(2, one_g1[0]), forward(3, one_g1[1])]

    def scale_of(buffers, count):
        def add(g, acc):
            span = pl.ds(pl.multiple_of(256 * g, 256), 256)
            for j in buffers:
                for c in range(2):
                    v = G[j, c, span].astype(f32).reshape(32, 8, 128)
                    acc = acc + jnp.sum(v * v, axis=0)
            return acc

        squares = lax.fori_loop(0, 9, add, jnp.zeros((8, 128), f32))
        return lax.rsqrt(jnp.sum(squares) / count + 1e-06)

    for copy in two_c[0] + two_c[1]:
        copy.wait_recv()
    scale_two = scale_of((0, 1), 9.0 * 256 * 512)

    @pl.loop(0, 9)
    def _(g):
        span = pl.ds(pl.multiple_of(256 * g, 256), 256)
        for c in range(2):
            for j in range(2):
                two[span, 256 * c + 128 * j : 256 * c + 128 * j + 128] = (G[j, c, span].astype(f32) * scale_two).astype(bf16)

    for copy in one_c[0] + one_c[1]:
        copy.wait_recv()
    scale_one = scale_of((2,), 9.0 * 256 * 256)

    @pl.loop(0, 9)
    def _(g):
        span = pl.ds(pl.multiple_of(256 * g, 256), 256)
        for c in range(2):
            one[span, 128 * c : 128 * c + 128] = (G[2, c, span].astype(f32) * scale_one).astype(bf16)

    for copy in pending:
        copy.wait_send()


def on_device(image, kernel_one, kernel_two, cotangent):
    vmem = pl.BlockSpec(memory_space=pltpu.VMEM)
    dma = pltpu.SemaphoreType.DMA
    pairs = [(8,), (3,), (8,), (3,), (3,), (4, 3), (4, 3), (3, 7), (3, 7), (4, 3), (4, 3), (4, 4)]
    scratch = [
        ((16, 128, 256), bf16), ((2304, 256), bf16), ((2304, 512), bf16), ((8, 64, 512), bf16),
        ((18, 2, 128, 128), f32), ((18, 128, 768), bf16), ((18, 128, 768), bf16),
        ((2, 2, 8, 64, 256), bf16), ((16, 128, 256), f32), ((9, 64, 512), bf16), ((9, 64, 512), bf16),
        ((2, 16, 256), f32), ((2, 16, 256), bf16), ((2, 128, 256), bf16), ((2, 3, 16, 256), bf16),
        ((16, 512), bf16), ((64, 512), bf16), ((2, 16, 512), bf16),
        ((2, 16, 256), bf16), ((2, 128, 256), bf16), ((2, 3, 16, 256), bf16),
        ((24, 256), f32), ((24, 256), f32),
        ((2, 2304, 256), bf16), ((2304, 256), bf16), ((2, 2304, 128), bf16), ((2304, 128), bf16),
        ((3, 2304, 128), bf16), ((3, 3, 576, 128), bf16), ((3, 576, 128), bf16), ((3, 3, 144, 128), bf16),
        ((3, 8, 32, 128), bf16), ((3, 8, 32, 128), bf16), ((3, 2, 2304, 128), bf16),
    ]
    image_grad, two, one = pl.pallas_call(
        kernel,
        out_shape=(
            jax.ShapeDtypeStruct((16, 128, 256), bf16),
            jax.ShapeDtypeStruct((2304, 512), bf16),
            jax.ShapeDtypeStruct((2304, 256), bf16),
        ),
        in_specs=[pl.BlockSpec(memory_space=pl.ANY)] * 4,
        out_specs=[vmem] * 3,
        scratch_shapes=[pltpu.VMEM(shape, kind) for shape, kind in scratch] + [dma((4,))] + [dma(s) for s in pairs for _ in range(2)],
        compiler_params=pltpu.CompilerParams(collective_id=0, has_side_effects=True, vmem_limit_bytes=60 << 20),
    )(image, kernel_one.reshape(2304, 256), kernel_two.reshape(2304, 512), cotangent)
    return image_grad, one.reshape(kernel_one.shape), two.reshape(kernel_two.shape)


def solution(mesh):
    placed = (P("row", "col", None), P(), P(), P("row", "col", None))
    return jax.shard_map(
        on_device, mesh=mesh, in_specs=placed, out_specs=(P("row", "col", None), P(), P()), check_vma=False
    )
```

time: 441 us -> 80.9 us (0.18)
  waiting for transfers between devices: 262 us -> 0 us
  Pallas kernels: 0 us -> 73.9 us
  local copies, waits for them, and re-layouts: 74.6 us -> 6.21 us
  starting transfers between devices: 34 us -> 0 us
  other arithmetic: 28 us -> 0 us
  matrix products: 24.6 us -> 0 us
  between operations: 16.2 us -> 0.65 us
    psum x1 -> x0, waiting for transfers between devices: 254 us -> none  [on_device(): total_one, total_two = lax.psum((flat_one, flat_two), ('row', 'col'))]
    pallas_call x0 -> x1, Pallas kernels: none -> 73.9 us  [on_device(): pl.pallas_call(kernel, out_shape=(jax.ShapeDtypeStruct((16, 128, 256), bf...]
    ppermute x12 -> x0, starting transfers between devices: 33.9 us -> none  [the longest x4 14.7 us: passed_along(): return lax.ppermute(shard, axis, pairs)]
    slice x17 -> x0, local copies, waits for them, and re-layouts: 27.2 us -> none  [the longest x9 19.8 us: on_device(): act_pad[row_off:row_off + rows_here - 1:2, col_off:col_off + cols_here -...]
    dot_general x18 -> x0, matrix products: 17.1 us -> none  [the longest x9 11.4 us: on_device(): jnp.einsum('ijc,ije->ce', patch, cotangent, preferred_element_type=jnp.fl...]
    conv_general_dilated x12 -> x0, local copies, waits for them, and re-layouts: 15.6 us -> none  [conv_local(): lax.conv_general_dilated(source[None], kernel, (1, 1), padding, lhs_dilat...]
    unnamed x62 -> x5, local copies, waits for them, and re-layouts: 19 us -> 6.21 us
    ppermute x12 -> x0, waiting for transfers between devices: 7.78 us -> none  [the longest x4 7.75 us: padded(): after = lax.ppermute(initial, axis, down)]
  transfers between devices with their start and end apart: 13 -> 0, of which waited for: 4 -> 0; matrix products, arithmetic and copies ran while one was open for 13% -> 0% of each run, Pallas kernels for 0% -> 0%
where the time goes in v1:
time: 80.9 us; the launch traced here: 80.8 us
  Pallas kernels  73.9 us (91%)
  local copies, waits for them, and re-layouts  6.21 us (8%)
    pallas_call x1, Pallas kernels, on_device(): pl.pallas_call(kernel, out_shape=(jax.ShapeDtypeStruct((16, 128, 256), bf...  73.9 us
    unnamed x5, local copies, waits for them, and re-layouts  6.21 us

profile of v1, /device:TPU:1, one launch (start us, length us, event | category | flops | bytes accessed | tf_op | source)
XLA Modules:
  0.0 80.8 jit_solution(15891337968168694183)
XLA Ops:
  0.6 73.9 %shard_map.67 = (bf16[16,128,256]{2,1,0:T(8,128)(2,1)}, bf16[2304,512]{1,0:T(8,128)(2,1)}, bf16[2304,256]{1,0:T(8,128)(2,1)}) custom-call(bf16[16,128,256]{2,1,0:T(8,128)(2,1)} %image_hbm.1, bf16[2304,256]{1,0:T(8,128)(2,1)} %bitcast.6, bf16[2304,512]{1,0:T(8,128)(2,1)} %bitcast.4, bf16[8,64,512]{2,1,0:T(8,128)(2,1)} %cot_hbm.1), custom_call_target="tpu_custom_call" | custom-call | tf_op jit(solution)/shard_map/pallas_call | solution.py:458
  74.6 0.0 copy-start
  74.6 2.4 %copy.10 = bf16[16,128,256]{2,1,0:T(8,128)(2,1)} copy(bf16[16,128,256]{2,1,0:T(8,128)(2,1)} %get-tuple-element.12) | data formatting | bytes 2097152
  77.0 2.4 %copy.11 = bf16[3,3,256,256]{3,2,1,0:T(8,128)(2,1)} copy(bf16[3,3,256,256]{3,2,1,0:T(8,128)(2,1)} %bitcast.7) | data formatting | bytes 2359296
  79.4 0.0 copy-done
  79.4 1.4 %copy.12 = bf16[3,3,256,512]{3,2,1,0:T(8,128)(2,1)} copy(bf16[3,3,256,512]{3,2,1,0:T(8,128)(2,1)S(1)} %bitcast.5) | data formatting | bytes 4718592
Async XLA Ops:
  74.6 4.8 %copy-start = (bf16[2304,512]{1,0:T(8,128)(2,1)S(1)}, bf16[2304,512]{1,0:T(8,128)(2,1)}, u32[]{:S(2)}) copy-start(bf16[2304,512]{1,0:T(8,128)(2,1)} %get-tuple-element.8) | copy-start | bytes 7077892

commit v2 on v1

v2 whole, which is shorter than its diff:
```python
import functools

import jax
import jax.numpy as jnp
from jax import lax
from jax.experimental import pallas as pl
from jax.experimental.pallas import tpu as pltpu
from jax.sharding import PartitionSpec as P

MESH = pl.DeviceIdType.MESH
bf16, f32 = jnp.bfloat16, jnp.float32
ROWS, COLS = 32, 8
NX, NY, NZ = 4, 4, 8
JOBS = (
    (0, 0, 1280, "yx"), (1, 0, 1024, "xy"),
    (0, 1280, 1024, "yx"), (1, 1024, 1280, "xy"),
    (2, 0, 1280, "yx"), (2, 1280, 1024, "xy"),
)


def dot(a, b):
    return jnp.dot(a, b, preferred_element_type=f32)


def dot_nt(a, b):
    return lax.dot_general(a, b, (((1,), (1,)), ((), ())), preferred_element_type=f32)


def dot_tn(a, b):
    return lax.dot_general(a, b, (((0,), (0,)), ((), ())), preferred_element_type=f32)


def total_of(terms):
    return functools.reduce(lambda u, v: u + v, terms)


def kernel(
    image_hbm, k1_hbm, k2_hbm, cot_hbm,
    image_grad, G, squares,
    image, k1, k2, cot, F, X, V, A, D, B, C, Cs,
    edge32, edges, hrow, hcol, cedge, crow, ccol, pedges, prow, pcol, left, right, fixes,
    T2, R2, T1, R1, S, P1, Q1, P2, Zs, Zr,
    load_sem,
    img_s, img_r, cot_s, cot_r, pg_s, pg_r, c2_s, c2_r, c1_s, c1_r,
    a1_s, a1_r, a2_s, a2_r, az_s, az_r, gz_s, gz_r, g2_s, g2_r, g1_s, g1_r, gc_s, gc_r,
):
    row, col = lax.axis_index("row"), lax.axis_index("col")
    z, x, y, core = row // NX, row % NX, col // 2, col % 2
    other = 1 - core

    def at_row(d):
        return (row + d + ROWS) % ROWS

    def at_col(d):
        return (col + d + COLS) % COLS

    def at_x(k):
        return (z * NX + (x + k) % NX, col)

    def at_y(k):
        return (row, ((y + k) % NY) * 2 + core)

    def at_z(k):
        return (((z + k) % NZ) * NX + x, col)

    sibling = (row, y * 2 + other)
    around = [(at_row(u), at_col(v)) for u in (-1, 0, 1) for v in (-1, 0, 1) if (u, v) != (0, 0)]
    pending = []

    def send(src, dst, send_sem, recv_sem, to):
        copy = pltpu.make_async_remote_copy(
            src_ref=src, dst_ref=dst, send_sem=send_sem, recv_sem=recv_sem, device_id=to, device_id_type=MESH
        )
        copy.start()
        pending.append(copy)
        return copy

    loads = []
    for n, (src, dst) in enumerate(((image_hbm, image), (cot_hbm, cot), (k1_hbm, k1), (k2_hbm, k2))):
        copy = pltpu.make_async_copy(src, dst, load_sem.at[n])
        copy.start()
        loads.append(copy)

    barrier = pltpu.get_barrier_semaphore()
    greeted = around + [sibling] + [at_y(k) for k in (1, 2, 3)] + [at_x(k) for k in (1, 2, 3)] + [at_z(k) for k in range(1, NZ)]
    for to in greeted:
        pl.semaphore_signal(barrier, inc=1, device_id=to, device_id_type=MESH)

    def spread(slot, values):
        v = values.astype(f32)
        F[slot, 0] = v[:, :128]
        F[slot, 1] = v[:, 128:]

    loads[0].wait()

    @pl.loop(0, 16)
    def _(p):
        spread(p, image[p])

    for p in range(16):
        for h in range(2):
            edge32[0, p : p + 1, 128 * h : 128 * h + 128] = F[p, h, 0:1, :]
            edge32[1, p : p + 1, 128 * h : 128 * h + 128] = F[p, h, 127:128, :]
    edges[...] = edge32[...].astype(bf16)

    first_at = lax.broadcasted_iota(jnp.int32, (64, 256), 0) == 0
    last_at = lax.broadcasted_iota(jnp.int32, (64, 256), 0) == 63

    def shifted(ref, r, even, odd, before_first, after_last, centre):
        before = jnp.where(first_at, before_first, pltpu.roll(odd, 1, 0)).astype(bf16)
        after = jnp.where(last_at, after_last, pltpu.roll(even, 63, 0)).astype(bf16)
        e, o = even.astype(bf16), odd.astype(bf16)
        ref[r, 0:64, 0:256] = before
        ref[r, 64:128, 0:256] = e
        if centre:
            ref[r, 0:64, 256:512] = e
            ref[r, 64:128, 256:512] = o
        ref[r, 0:64, 512:768] = o
        ref[r, 64:128, 512:768] = after

    def columns_of(slot, odd):
        return jnp.concatenate([F[slot, h, pl.ds(odd, 64, stride=2), :] for h in (0, 1)], axis=1)

    @pl.loop(0, 16)
    def _(p):
        shifted(X, p + 1, columns_of(p, 0), columns_of(p, 1), 0.0, 0.0, True)

    X[0] = jnp.zeros((128, 768), bf16)
    X[17] = jnp.zeros((128, 768), bf16)

    loads[1].wait()
    edge2 = [cot[i, 0:16, :].astype(f32)[0:1] for i in range(8)]
    cedge[...] = jnp.concatenate(edge2 + [jnp.zeros((8, 512), f32)], axis=0).astype(bf16)
    pl.semaphore_wait(barrier, len(greeted))

    def send_halos(first, last, ends, rows_to, cols_to, send_sem, recv_sem):
        sent = [
            send(first, rows_to.at[1], send_sem.at[0], recv_sem.at[0], (at_row(-1), col)),
            send(last, rows_to.at[0], send_sem.at[1], recv_sem.at[1], (at_row(1), col)),
        ]
        n = 2
        for side, v in ((1, -1), (0, 1)):
            for place, u in ((0, 1), (1, 0), (2, -1)):
                to = (at_row(u) if u else row, at_col(v))
                sent.append(send(ends.at[1 - side], cols_to.at[side, place], send_sem.at[n], recv_sem.at[n], to))
                n += 1
        return sent

    halo = send_halos(image.at[0], image.at[15], edges, hrow, hcol, img_s, img_r)
    cot_halo = [
        send(cot.at[0], crow, cot_s.at[0], cot_r.at[0], (at_row(-1), col)),
        send(cedge, ccol.at[0], cot_s.at[1], cot_r.at[1], (row, at_col(-1))),
        send(cedge, ccol.at[1], cot_s.at[2], cot_r.at[2], (at_row(-1), at_col(-1))),
    ]

    end_at = lax.broadcasted_iota(jnp.int32, (64, 512), 0) == 63
    for i in range(8):
        C[i] = cot[i]
        Cs[i] = jnp.where(end_at, 0.0, pltpu.roll(cot[i].astype(f32), 63, 0)).astype(bf16)
    C[8] = jnp.zeros((64, 512), bf16)
    Cs[8] = jnp.zeros((64, 512), bf16)

    loads[2].wait()

    @pl.loop(0, 4)
    def _(g):
        acc = total_of(
            [dot(X[pl.ds(4 * g + a, 4)].reshape(512, 768), k1[768 * a : 768 * a + 768, :]) for a in range(3)]
        )
        D[pl.ds(4 * g, 4)] = acc.reshape(4, 128, 256)

    loads[3].wait()

    def tap(a, b):
        return k2[(3 * a + b) * 256 : (3 * a + b) * 256 + 256, :]

    @pl.loop(0, 2)
    def _(g):
        for rp in range(2):
            for cp in range(2):
                terms = []
                for a, d in ((1, 0),) if rp == 0 else ((2, 0), (0, 1)):
                    for b, ref in ((1, C),) if cp == 0 else ((2, C), (0, Cs)):
                        terms.append(dot_nt(ref[pl.ds(4 * g + d, 4)].reshape(256, 512), tap(a, b)))
                acc = total_of(terms).reshape(4, 64, 256)
                for u in range(4):
                    B[2 * (4 * g + u) + rp, 64 * cp : 64 * cp + 64] = acc[u]

    def sides_of(cols_to):
        for side, ref, none in ((0, left, col == 0), (1, right, col == COLS - 1)):
            above = jnp.where((row == 0) | none, 0.0, cols_to[side, 0].astype(f32)[15:16])
            mid = jnp.where(none, 0.0, cols_to[side, 1].astype(f32))
            below = jnp.where((row == ROWS - 1) | none, 0.0, cols_to[side, 2].astype(f32)[0:1])
            ref[0:1] = above
            ref[1:17] = mid
            ref[17:18] = below

    for copy in halo:
        copy.wait_recv()
    sides_of(hcol)
    spread(16, jnp.where(row == 0, 0.0, hrow[0].astype(f32)))
    spread(17, jnp.where(row == ROWS - 1, 0.0, hrow[1].astype(f32)))
    for slot, r in ((16, 0), (17, 17)):
        shifted(X, r, columns_of(slot, 0), columns_of(slot, 1), left[r : r + 1], right[r : r + 1], True)
    top_at = lax.broadcasted_iota(jnp.int32, (16, 256), 0) == 0
    low_at = lax.broadcasted_iota(jnp.int32, (16, 256), 0) == 15
    for r in range(1, 17):
        X[r, 0:16, 0:256] = jnp.where(top_at, left[r : r + 1], X[r, 0:16, 0:256].astype(f32)).astype(bf16)
        X[r, 112:128, 512:768] = jnp.where(low_at, right[r : r + 1], X[r, 112:128, 512:768].astype(f32)).astype(bf16)
    D[0] += dot(X[0], k1[0:768, :])
    D[15] += dot(X[17], k1[1536:2304, :])
    for side, ref, b in ((0, left, 0), (1, right, 2)):
        ref[0:1] = jnp.zeros((1, 256), f32)
        ref[17:18] = jnp.zeros((1, 256), f32)
        fixes[side] = total_of(
            [dot(ref[a : a + 16].astype(bf16), k1[(3 * a + b) * 256 : (3 * a + b) * 256 + 256, :]) for a in range(3)]
        )
        at = 127 * side
        for p in range(16):
            D[p, at : at + 1] += fixes[side, p : p + 1]

    for copy in cot_halo:
        copy.wait_recv()
    no_right, no_below = col == COLS - 1, row == ROWS - 1
    beside = jnp.where(no_right, 0.0, ccol[0].astype(f32))
    corner = jnp.where(no_right | no_below, 0.0, ccol[1].astype(f32)[0:1])
    under = jnp.where(no_below, 0.0, crow[...].astype(f32))
    C[8] = under.astype(bf16)
    Cs[8] = jnp.where(end_at, corner, pltpu.roll(under, 63, 0)).astype(bf16)
    foot_at = lax.broadcasted_iota(jnp.int32, (16, 512), 0) == 15
    for i in range(8):
        Cs[i, 48:64] = jnp.where(foot_at, beside[i : i + 1], Cs[i, 48:64].astype(f32)).astype(bf16)
    B[15, 0:64] += dot_nt(C[8], tap(0, 1))
    B[15, 64:128] += dot_nt(C[8], tap(0, 2)) + dot_nt(Cs[8], tap(0, 0))
    for a in range(3):
        fixes[a] = dot_nt(beside.astype(bf16), tap(a, 0))
    for i in range(8):
        B[2 * i, 127:128] += fixes[1, i : i + 1]
        below = fixes[2, i : i + 1]
        B[2 * i + 1, 127:128] += below + fixes[0, i + 1 : i + 2] if i < 7 else below

    @pl.loop(0, 8)
    def _(i):
        for rp in range(2):
            pre = D[2 * i + rp]
            s = jax.nn.sigmoid(pre)
            act = (pre * s).astype(bf16)
            for c in range(2):
                A[rp, c, i] = act[64 * c : 64 * c + 64]
            V[2 * i + rp + 1, :, 256:512] = (B[2 * i + rp] * s * (1.0 + pre * (1.0 - s))).astype(bf16)

    for p in range(16):
        edge32[0, p : p + 1] = V[p + 1, 0:16, 256:512].astype(f32)[0:1]
        edge32[1, p : p + 1] = V[p + 1, 112:128, 256:512].astype(f32)[15:16]
    pedges[...] = edge32[...].astype(bf16)
    pg_halo = send_halos(V.at[1, :, 256:512], V.at[16, :, 256:512], pedges, prow, pcol, pg_s, pg_r)

    def axis_of(name):
        return (y, at_y, NY) if name == "y" else (x, at_x, NX)

    def places(job):
        j, base, rows, order = job
        place = JOBS.index(job)
        first = JOBS[place - 1][2] if place % 2 else 0
        o1, o2 = first // 4, first // 16
        return j, base, rows // 4, rows // 16, o1, o2, axis_of(order[0]), axis_of(order[1])

    def spans(job):
        j, base, n1, n2, o1, o2, (i1, _, _), (i2, _, _) = places(job)
        return base + n1 * i1, base + n1 * i1 + n2 * i2

    def al(v):
        return pl.multiple_of(v, 16)

    def stage1(n):
        j, base, n1, n2, o1, o2, (i1, to, _), _ = places(JOBS[n])
        return [
            send(
                S.at[j, pl.ds(al(base + n1 * ((i1 + k) % 4)), n1)], P1.at[n // 2, k - 1, pl.ds(o1, n1)],
                a1_s.at[n, k - 1], a1_r.at[n, k - 1], to(k),
            )
            for k in (1, 2, 3)
        ]

    def stage2(n, arrived):
        j, base, n1, n2, o1, o2, (i1, _, _), (i2, to, _) = places(JOBS[n])
        for copy in arrived:
            copy.wait_recv()
        own = S[j, pl.ds(al(base + n1 * i1), n1)].astype(f32)
        Q1[n // 2, o1 : o1 + n1] = total_of([own] + [P1[n // 2, k, o1 : o1 + n1].astype(f32) for k in range(3)]).astype(bf16)
        return [
            send(
                Q1.at[n // 2, pl.ds(al(o1 + n2 * ((i2 + k) % 4)), n2)], P2.at[n // 2, k - 1, pl.ds(o2, n2)],
                a2_s.at[n, k - 1], a2_r.at[n, k - 1], to(k),
            )
            for k in (1, 2, 3)
        ]

    def stage_z(j, arrived):
        for copy in arrived:
            copy.wait_recv()
        for n in (2 * j, 2 * j + 1):
            _, base, n1, n2, o1, o2, _, (i2, _, _) = places(JOBS[n])
            own = Q1[j, pl.ds(al(o1 + n2 * i2), n2)].astype(f32)
            summed = total_of([own] + [P2[j, k, o2 : o2 + n2].astype(f32) for k in range(3)]).astype(bf16)
            for u in range(n2 // 16):
                unit = o2 // 16 + u
                block = summed[16 * u : 16 * u + 16]
                if unit < NZ:
                    Zs[j, unit, 0:16] = block
                else:
                    for k in range(NZ):
                        Zs[j, k, 16:32] = block
        Zr[j, z] = Zs[j, z]
        return [send(Zs.at[j, (z + k) % NZ], Zr.at[j, z], az_s.at[j, k - 1], az_r.at[j, k - 1], at_z(k)) for k in range(1, NZ)]

    def unit_at(g, unit):
        units = JOBS[2 * g][2] // 256
        return spans(JOBS[2 * g])[1] + 16 * unit, spans(JOBS[2 * g + 1])[1] + 16 * (unit - units), (unit + 8 - units) // 8

    def gather_z(g, arrived):
        for copy in arrived:
            copy.wait_recv()
        summed = total_of([Zr[g, k].astype(f32) for k in range(NZ)]).astype(bf16)
        in_first, in_second, second = unit_at(g, z)
        j0, j1 = JOBS[2 * g][0], JOBS[2 * g + 1][0]
        j = j0 + second * (j1 - j0)
        mine = pl.ds(al((1 - second) * in_first + second * in_second), 16)
        G[j, core, mine] = summed[0:16]
        G[j1, core, pl.ds(al(unit_at(g, NZ)[1]), 16)] = summed[16:32]
        here = G.at[j, core, mine]
        return [send(here, here, gz_s.at[g, k - 1], gz_r.at[g, k - 1], at_z(k)) for k in range(1, NZ)]

    def gather2(n, arrived):
        j, base, n1, n2, o1, o2, _, (i2, to, _) = places(JOBS[n])
        for copy in arrived:
            copy.wait_recv()
        here = G.at[j, core, pl.ds(al(spans(JOBS[n])[1]), n2)]
        return [send(here, here, g2_s.at[n, k - 1], g2_r.at[n, k - 1], to(k)) for k in (1, 2, 3)]

    def to_sibling(n, k):
        j, base, n1, n2, o1, o2, (i1, _, _), _ = places(JOBS[n])
        here = G.at[j, core, pl.ds(al(base + n1 * ((i1 - k + 4) % 4)), n1)]
        return send(here, here, gc_s.at[n, k], gc_r.at[n, k], sibling)

    def gather1(n, arrived):
        j, base, n1, n2, o1, o2, (i1, to, _), _ = places(JOBS[n])
        for copy in arrived:
            copy.wait_recv()
        here = G.at[j, core, pl.ds(al(spans(JOBS[n])[0]), n1)]
        sent = [send(here, here, g1_s.at[n, k - 1], g1_r.at[n, k - 1], to(k)) for k in (1, 2, 3)]
        return sent, [to_sibling(n, 0)]

    def forward(n, arrived):
        sent, across = arrived
        for k in (1, 2, 3):
            sent[k - 1].wait_recv()
            across.append(to_sibling(n, k))
        return across

    def two_taps(first_tap, last_tap, n):
        for m in range(first_tap, last_tap):
            a, b = m // 3, m % 3
            first = 1 if a == 0 else 0
            lhs = A[(a + 1) % 2, (b + 1) % 2].reshape(512, 256)
            rhs = (Cs if b == 0 else C)[first : first + 8].reshape(512, 512)
            out = dot_tn(lhs, rhs).astype(bf16)
            for h in range(2):
                T2[h, 256 * m : 256 * m + 256, :] = out[:, 256 * h : 256 * h + 256]
        span = pl.ds(256 * first_tap, 256 * (last_tap - first_tap))
        return send(T2.at[other, span], R2.at[span], c2_s.at[n], c2_r.at[n], sibling)

    def both_two(copies, first_tap, last_tap):
        for copy in copies:
            copy.wait_recv()

        @pl.loop(first_tap, last_tap)
        def _(g):
            span = pl.ds(pl.multiple_of(256 * g, 256), 256)
            both = T2[core, span].astype(f32) + R2[span].astype(f32)
            S[0, span] = both[:, :128].astype(bf16)
            S[1, span] = both[:, 128:].astype(bf16)

    def one_taps(a):
        for b in range(3):
            lhs = X[a : a + 16, :, 256 * b : 256 * b + 256].reshape(2048, 256)
            out = dot_tn(lhs, V[1:17, :, 256:512].reshape(2048, 256)).astype(bf16)
            for h in range(2):
                T1[h, (3 * a + b) * 256 : (3 * a + b) * 256 + 256, :] = out[:, 128 * h : 128 * h + 128]
        span = pl.ds(768 * a, 768)
        return send(T1.at[other, span], R1.at[span], c1_s.at[a], c1_r.at[a], sibling)

    core_two = [two_taps(0, 3, 0), two_taps(3, 5, 1), two_taps(5, 7, 2), two_taps(7, 9, 3)]
    both_two(core_two[:2], 0, 5)
    g0 = [stage1(0), stage1(1)]
    core_one = [one_taps(0)]
    both_two(core_two[2:], 5, 9)
    g1 = [stage1(2), stage1(3)]
    core_one += [one_taps(1), one_taps(2)]

    for copy in pg_halo:
        copy.wait_recv()
    sides_of(pcol)

    @pl.loop(0, 16)
    def _(p):
        shifted(
            V, p + 1, V[p + 1, 0:64, 256:512].astype(f32), V[p + 1, 64:128, 256:512].astype(f32),
            left[pl.ds(p + 1, 1)], right[pl.ds(p + 1, 1)], False,
        )

    for place, r, none in ((0, 0, row == 0), (1, 17, row == ROWS - 1)):
        values = jnp.where(none, 0.0, prow[place].astype(f32))
        shifted(V, r, values[0:64], values[64:128], left[r : r + 1], right[r : r + 1], True)

    for copy in core_one:
        copy.wait_recv()

    @pl.loop(0, 9)
    def _(g):
        span = pl.ds(pl.multiple_of(256 * g, 256), 256)
        S[2, span] = (T1[core, span].astype(f32) + R1[span].astype(f32)).astype(bf16)

    g2 = [stage1(4), stage1(5)]

    def image_rows(g):
        terms = []
        for a in range(3):
            for b in range(3):
                m = 3 * (2 - a) + (2 - b)
                lhs = V[pl.ds(4 * g + a, 4), :, 256 * b : 256 * b + 256].reshape(512, 256)
                terms.append(dot_nt(lhs, k1[256 * m : 256 * m + 256, :]))
        acc = total_of(terms).reshape(4, 128, 256)
        for u in range(4):
            p = 4 * g + u
            for h in range(2):
                F[p, h, pl.ds(0, 64, stride=2), :] = acc[u, 0:64, 128 * h : 128 * h + 128]
                F[p, h, pl.ds(1, 64, stride=2), :] = acc[u, 64:128, 128 * h : 128 * h + 128]
            image_grad[p] = jnp.concatenate([F[p, 0], F[p, 1]], axis=1).astype(bf16)

    pl.loop(0, 4)(image_rows)

    def pair(step, g, arrived):
        return [step(2 * g, arrived[0]), step(2 * g + 1, arrived[1])]

    def both(arrived):
        return arrived[0] + arrived[1]

    def arrive(across):
        for copy in both(across):
            copy.wait_recv()

    g0 = pair(stage2, 0, g0)
    g1 = pair(stage2, 1, g1)
    g0 = stage_z(0, both(g0))
    g2 = pair(stage2, 2, g2)
    g1 = stage_z(1, both(g1))
    g0 = gather_z(0, g0)
    g2 = stage_z(2, both(g2))
    g1 = gather_z(1, g1)
    g0 = pair(gather2, 0, [g0, []])
    g2 = gather_z(2, g2)
    g1 = pair(gather2, 1, [g1, []])
    g0 = pair(gather1, 0, g0)
    g2 = pair(gather2, 2, [g2, []])
    g1 = pair(gather1, 1, g1)
    g2 = pair(gather1, 2, g2)
    g0 = pair(forward, 0, g0)
    g1 = pair(forward, 1, g1)

    def squares_of(buffers):
        def add(g, acc):
            span = pl.ds(pl.multiple_of(256 * g, 256), 256)
            for j in buffers:
                for c in range(2):
                    v = G[j, c, span].astype(f32).reshape(32, 8, 128)
                    acc = acc + jnp.sum(v * v, axis=0)
            return acc

        return lax.fori_loop(0, 9, add, jnp.zeros((8, 128), f32))

    arrive(g0)
    arrive(g1)
    squares[0] = squares_of((0, 1))
    g2 = pair(forward, 2, g2)
    arrive(g2)
    squares[1] = squares_of((2,))

    for copy in pending:
        copy.wait_send()


def scaled(rows, G, squares, image_grad, two, one, two_v, one_v, sem):
    copies = [pltpu.make_async_copy(rows, image_grad, sem.at[0])]
    copies[0].start()
    scale = [lax.rsqrt(jnp.sum(squares[n]) / count + 1e-06) for n, count in ((0, 9.0 * 256 * 512), (1, 9.0 * 256 * 256))]
    for a in range(3):
        span = pl.ds(768 * a, 768)
        for c in range(2):
            for j in range(2):
                two_v[span, 256 * c + 128 * j : 256 * c + 128 * j + 128] = (G[j, c, span].astype(f32) * scale[0]).astype(bf16)
            one_v[span, 128 * c : 128 * c + 128] = (G[2, c, span].astype(f32) * scale[1]).astype(bf16)
        for n, (src, dst) in enumerate(((two_v, two), (one_v, one))):
            copies.append(pltpu.make_async_copy(src.at[span], dst.at[span], sem.at[1 + 2 * a + n]))
            copies[-1].start()
    for copy in copies:
        copy.wait()


def on_device(image, kernel_one, kernel_two, cotangent):
    vmem = pl.BlockSpec(memory_space=pltpu.VMEM)
    hbm = pl.BlockSpec(memory_space=pl.ANY)
    dma = pltpu.SemaphoreType.DMA
    pairs = [(8,), (3,), (8,), (4,), (3,), (6, 3), (6, 3), (3, 7), (3, 7), (6, 3), (6, 3), (6, 4)]
    scratch = [
        ((16, 128, 256), bf16), ((2304, 256), bf16), ((2304, 512), bf16), ((8, 64, 512), bf16),
        ((18, 2, 128, 128), f32), ((18, 128, 768), bf16), ((18, 128, 768), bf16),
        ((2, 2, 8, 64, 256), bf16), ((16, 128, 256), f32), ((16, 128, 256), f32), ((9, 64, 512), bf16), ((9, 64, 512), bf16),
        ((2, 16, 256), f32), ((2, 16, 256), bf16), ((2, 128, 256), bf16), ((2, 3, 16, 256), bf16),
        ((16, 512), bf16), ((64, 512), bf16), ((2, 16, 512), bf16),
        ((2, 16, 256), bf16), ((2, 128, 256), bf16), ((2, 3, 16, 256), bf16),
        ((24, 256), f32), ((24, 256), f32), ((3, 16, 256), f32),
        ((2, 2304, 256), bf16), ((2304, 256), bf16), ((2, 2304, 128), bf16), ((2304, 128), bf16),
        ((3, 2304, 128), bf16), ((3, 3, 576, 128), bf16), ((3, 576, 128), bf16), ((3, 3, 144, 128), bf16),
        ((3, 8, 32, 128), bf16), ((3, 8, 32, 128), bf16),
    ]
    kept = [pltpu.VMEM((16, 128, 256), bf16), pltpu.VMEM((3, 2, 2304, 128), bf16), pltpu.VMEM((2, 8, 128), f32)]
    rows, sums, squares = pl.pallas_call(
        kernel,
        out_shape=kept,
        in_specs=[hbm] * 4,
        out_specs=[vmem] * 3,
        scratch_shapes=[pltpu.VMEM(shape, kind) for shape, kind in scratch] + [dma((4,))] + [dma(s) for s in pairs for _ in range(2)],
        compiler_params=pltpu.CompilerParams(collective_id=0, has_side_effects=True, vmem_limit_bytes=50 << 20),
    )(image, kernel_one.reshape(2304, 256), kernel_two.reshape(2304, 512), cotangent)
    image_grad, two, one = pl.pallas_call(
        scaled,
        out_shape=(
            jax.ShapeDtypeStruct((16, 128, 256), bf16),
            jax.ShapeDtypeStruct((2304, 512), bf16),
            jax.ShapeDtypeStruct((2304, 256), bf16),
        ),
        in_specs=[vmem] * 3,
        out_specs=[hbm] * 3,
        scratch_shapes=[pltpu.VMEM((2304, 512), bf16), pltpu.VMEM((2304, 256), bf16), dma((7,))],
        compiler_params=pltpu.CompilerParams(vmem_limit_bytes=16 << 20),
    )(rows, sums, squares)
    return image_grad, one.reshape(kernel_one.shape), two.reshape(kernel_two.shape)


def solution(mesh):
    placed = (P("row", "col", None), P(), P(), P("row", "col", None))
    return jax.shard_map(
        on_device, mesh=mesh, in_specs=placed, out_specs=(P("row", "col", None), P(), P()), check_vma=False
    )
```

time: 80.9 us -> 70.3 us (0.87)
  local copies, waits for them, and re-layouts: 6.21 us -> 0 us
  Pallas kernels: 73.9 us -> 69.6 us
    unnamed x5 -> x0, local copies, waits for them, and re-layouts: 6.21 us -> none
    pallas_call x1 -> x2, Pallas kernels: 73.9 us -> 69.6 us  [the longest x1 67.4 us: on_device(): pl.pallas_call(kernel, out_shape=kept, in_specs=[hbm] * 4, out_specs=[vme...]
where the time goes in v2:
time: 70.3 us; the launch traced here: 70.2 us
  Pallas kernels  69.6 us (99%)
    pallas_call x1, Pallas kernels, on_device(): pl.pallas_call(kernel, out_shape=kept, in_specs=[hbm] * 4, out_specs=[vme...  67.4 us
    pallas_call x1, Pallas kernels, on_device(): pl.pallas_call(scaled, out_shape=(jax.ShapeDtypeStruct((16, 128, 256), bf...  2.21 us

profile of v2, /device:TPU:1, one launch (start us, length us, event | category | flops | bytes accessed | tf_op | source)
XLA Modules:
  0.0 70.2 jit_solution(7573980337819623498)
XLA Ops:
  0.6 67.4 %shard_map.67 = (bf16[16,128,256]{2,1,0:T(8,128)(2,1)S(1)}, bf16[3,2,2304,128]{3,2,1,0:T(8,128)(2,1)S(1)}, f32[2,8,128]{2,1,0:T(8,128)S(1)}) custom-call(bf16[16,128,256]{2,1,0:T(8,128)(2,1)} %image_hbm.1, bf16[2304,256]{1,0:T(8,128)(2,1)} %bitcast.5, bf16[2304,512]{1,0:T(8,128)(2,1)} %bitcast.4, bf16[8,64,512]{2,1,0:T(8,128)(2,1)} %cot_hbm.1), custom_call_target="tpu_custom_call" | custom-call | tf_op jit(solution)/shard_map/pallas_call | solution.py:528
  68.0 2.2 %shard_map.68 = (bf16[16,128,256]{2,1,0:T(8,128)(2,1)}, bf16[2304,512]{1,0:T(8,128)(2,1)}, bf16[2304,256]{1,0:T(8,128)(2,1)}) custom-call(bf16[16,128,256]{2,1,0:T(8,128)(2,1)S(1)} %get-tuple-element.9.rows, bf16[3,2,2304,128]{3,2,1,0:T(8,128)(2,1)S(1)} %get-tuple-element.10.G, f32[2,8,128]{2,1,0:T(8,128)S(1)} %get-tuple-element.11.squares), custom_call_target="tpu_custom_call" | custom-call | tf_op jit(solution)/shard_map/pallas_call | solution.py:536

commit v3 on v2

--- a/solution.py
+++ b/solution.py
@@ -11,10 +11,12 @@
 bf16, f32 = jnp.bfloat16, jnp.float32
 ROWS, COLS = 32, 8
 NX, NY, NZ = 4, 4, 8
+NEAR, ALONG_Z = (2, 1, 3), (4, 3, 5, 2, 6, 1, 7)
 JOBS = (
     (0, 0, 1280, "yx"), (1, 0, 1024, "xy"),
     (0, 1280, 1024, "yx"), (1, 1024, 1280, "xy"),
-    (2, 0, 1280, "yx"), (2, 1280, 1024, "xy"),
+    (2, 0, 768, "yx"), (2, 768, 512, "xy"),
+    (2, 1280, 512, "yx"), (2, 1792, 512, "xy"),
 )
 
 
@@ -36,9 +38,9 @@
 
 def kernel(
     image_hbm, k1_hbm, k2_hbm, cot_hbm,
-    image_grad, G, squares,
+    image_grad, two, G, squares,
     image, k1, k2, cot, F, X, V, A, D, B, C, Cs,
-    edge32, edges, hrow, hcol, cedge, crow, ccol, pedges, prow, pcol, left, right, fixes,
+    edge32, edges, hrow, hcol, cedge, crow, ccol, pedges, plast, prow, pcol, left, right, fixes,
     T2, R2, T1, R1, S, P1, Q1, P2, Zs, Zr,
     load_sem,
     img_s, img_r, cot_s, cot_r, pg_s, pg_r, c2_s, c2_r, c1_s, c1_r,
@@ -230,15 +232,6 @@
     foot_at = lax.broadcasted_iota(jnp.int32, (16, 512), 0) == 15
     for i in range(8):
         Cs[i, 48:64] = jnp.where(foot_at, beside[i : i + 1], Cs[i, 48:64].astype(f32)).astype(bf16)
-    B[15, 0:64] += dot_nt(C[8], tap(0, 1))
-    B[15, 64:128] += dot_nt(C[8], tap(0, 2)) + dot_nt(Cs[8], tap(0, 0))
-    for a in range(3):
-        fixes[a] = dot_nt(beside.astype(bf16), tap(a, 0))
-    for i in range(8):
-        B[2 * i, 127:128] += fixes[1, i : i + 1]
-        below = fixes[2, i : i + 1]
-        B[2 * i + 1, 127:128] += below + fixes[0, i + 1 : i + 2] if i < 7 else below
-
     @pl.loop(0, 8)
     def _(i):
         for rp in range(2):
@@ -247,13 +240,7 @@
             act = (pre * s).astype(bf16)
             for c in range(2):
                 A[rp, c, i] = act[64 * c : 64 * c + 64]
-            V[2 * i + rp + 1, :, 256:512] = (B[2 * i + rp] * s * (1.0 + pre * (1.0 - s))).astype(bf16)
-
-    for p in range(16):
-        edge32[0, p : p + 1] = V[p + 1, 0:16, 256:512].astype(f32)[0:1]
-        edge32[1, p : p + 1] = V[p + 1, 112:128, 256:512].astype(f32)[15:16]
-    pedges[...] = edge32[...].astype(bf16)
-    pg_halo = send_halos(V.at[1, :, 256:512], V.at[16, :, 256:512], pedges, prow, pcol, pg_s, pg_r)
+            D[2 * i + rp] = s * (1.0 + pre * (1.0 - s))
 
     def axis_of(name):
         return (y, at_y, NY) if name == "y" else (x, at_x, NX)
@@ -279,7 +266,7 @@
                 S.at[j, pl.ds(al(base + n1 * ((i1 + k) % 4)), n1)], P1.at[n // 2, k - 1, pl.ds(o1, n1)],
                 a1_s.at[n, k - 1], a1_r.at[n, k - 1], to(k),
             )
-            for k in (1, 2, 3)
+            for k in NEAR
         ]
 
     def stage2(n, arrived):
@@ -293,50 +280,62 @@
                 Q1.at[n // 2, pl.ds(al(o1 + n2 * ((i2 + k) % 4)), n2)], P2.at[n // 2, k - 1, pl.ds(o2, n2)],
                 a2_s.at[n, k - 1], a2_r.at[n, k - 1], to(k),
             )
-            for k in (1, 2, 3)
+            for k in NEAR
         ]
 
-    def stage_z(j, arrived):
+    def units_of(g):
+        return JOBS[2 * g][2] // 256, JOBS[2 * g][2] // 256 + JOBS[2 * g + 1][2] // 256
+
+    def stage_z(g, arrived):
         for copy in arrived:
             copy.wait_recv()
-        for n in (2 * j, 2 * j + 1):
+        for n in (2 * g, 2 * g + 1):
             _, base, n1, n2, o1, o2, _, (i2, _, _) = places(JOBS[n])
-            own = Q1[j, pl.ds(al(o1 + n2 * i2), n2)].astype(f32)
-            summed = total_of([own] + [P2[j, k, o2 : o2 + n2].astype(f32) for k in range(3)]).astype(bf16)
+            own = Q1[g, pl.ds(al(o1 + n2 * i2), n2)].astype(f32)
+            summed = total_of([own] + [P2[g, k, o2 : o2 + n2].astype(f32) for k in range(3)]).astype(bf16)
             for u in range(n2 // 16):
                 unit = o2 // 16 + u
                 block = summed[16 * u : 16 * u + 16]
                 if unit < NZ:
-                    Zs[j, unit, 0:16] = block
+                    Zs[g, unit, 0:16] = block
                 else:
                     for k in range(NZ):
-                        Zs[j, k, 16:32] = block
-        Zr[j, z] = Zs[j, z]
-        return [send(Zs.at[j, (z + k) % NZ], Zr.at[j, z], az_s.at[j, k - 1], az_r.at[j, k - 1], at_z(k)) for k in range(1, NZ)]
-
-    def unit_at(g, unit):
-        units = JOBS[2 * g][2] // 256
-        return spans(JOBS[2 * g])[1] + 16 * unit, spans(JOBS[2 * g + 1])[1] + 16 * (unit - units), (unit + 8 - units) // 8
+                        Zs[g, k, 16:32] = block
+        for unit in range(units_of(g)[1], NZ):
+            Zs[g, unit, 0:16] = jnp.zeros((16, 128), bf16)
+        size = 32 if units_of(g)[1] > NZ else 16
+        Zr[g, z, 0:size] = Zs[g, z, 0:size]
+        return [
+            send(
+                Zs.at[g, (z + k) % NZ, pl.ds(0, size)], Zr.at[g, z, pl.ds(0, size)],
+                az_s.at[g, k - 1], az_r.at[g, k - 1], at_z(k),
+            )
+            for k in ALONG_Z
+        ]
 
     def gather_z(g, arrived):
         for copy in arrived:
             copy.wait_recv()
-        summed = total_of([Zr[g, k].astype(f32) for k in range(NZ)]).astype(bf16)
-        in_first, in_second, second = unit_at(g, z)
+        first, units = units_of(g)
+        size = 32 if units > NZ else 16
+        summed = total_of([Zr[g, k, 0:size].astype(f32) for k in range(NZ)]).astype(bf16)
         j0, j1 = JOBS[2 * g][0], JOBS[2 * g + 1][0]
+        at0, at1 = spans(JOBS[2 * g])[1], spans(JOBS[2 * g + 1])[1]
+        second, unused = (z + 8 - first) // 8, (z + 8 - units) // 8 if units < NZ else 0
+        mine = (1 - second) * (at0 + 16 * z) + (second - unused) * (at1 + 16 * (z - first)) + unused * (2304 + 128 * (g % 2) + 16 * z)
         j = j0 + second * (j1 - j0)
-        mine = pl.ds(al((1 - second) * in_first + second * in_second), 16)
-        G[j, core, mine] = summed[0:16]
-        G[j1, core, pl.ds(al(unit_at(g, NZ)[1]), 16)] = summed[16:32]
-        here = G.at[j, core, mine]
-        return [send(here, here, gz_s.at[g, k - 1], gz_r.at[g, k - 1], at_z(k)) for k in range(1, NZ)]
+        G[j, core, pl.ds(al(mine), 16)] = summed[0:16]
+        if units > NZ:
+            G[j1, core, pl.ds(al(at1 + 16 * (NZ - first)), 16)] = summed[16:32]
+        here = G.at[j, core, pl.ds(al(mine), 16)]
+        return [send(here, here, gz_s.at[g, k - 1], gz_r.at[g, k - 1], at_z(k)) for k in ALONG_Z]
 
     def gather2(n, arrived):
         j, base, n1, n2, o1, o2, _, (i2, to, _) = places(JOBS[n])
         for copy in arrived:
             copy.wait_recv()
         here = G.at[j, core, pl.ds(al(spans(JOBS[n])[1]), n2)]
-        return [send(here, here, g2_s.at[n, k - 1], g2_r.at[n, k - 1], to(k)) for k in (1, 2, 3)]
+        return [send(here, here, g2_s.at[n, k - 1], g2_r.at[n, k - 1], to(k)) for k in NEAR]
 
     def to_sibling(n, k):
         j, base, n1, n2, o1, o2, (i1, _, _), _ = places(JOBS[n])
@@ -348,13 +347,13 @@
         for copy in arrived:
             copy.wait_recv()
         here = G.at[j, core, pl.ds(al(spans(JOBS[n])[0]), n1)]
-        sent = [send(here, here, g1_s.at[n, k - 1], g1_r.at[n, k - 1], to(k)) for k in (1, 2, 3)]
+        sent = [send(here, here, g1_s.at[n, k - 1], g1_r.at[n, k - 1], to(k)) for k in NEAR]
         return sent, [to_sibling(n, 0)]
 
     def forward(n, arrived):
         sent, across = arrived
-        for k in (1, 2, 3):
-            sent[k - 1].wait_recv()
+        for i, k in enumerate(NEAR):
+            sent[i].wait_recv()
             across.append(to_sibling(n, k))
         return across
 
@@ -381,22 +380,58 @@
             S[0, span] = both[:, :128].astype(bf16)
             S[1, span] = both[:, 128:].astype(bf16)
 
-    def one_taps(a):
-        for b in range(3):
+    def one_taps(first_tap, last_tap, n):
+        for m in range(first_tap, last_tap):
+            a, b = m // 3, m % 3
             lhs = X[a : a + 16, :, 256 * b : 256 * b + 256].reshape(2048, 256)
             out = dot_tn(lhs, V[1:17, :, 256:512].reshape(2048, 256)).astype(bf16)
             for h in range(2):
-                T1[h, (3 * a + b) * 256 : (3 * a + b) * 256 + 256, :] = out[:, 128 * h : 128 * h + 128]
-        span = pl.ds(768 * a, 768)
-        return send(T1.at[other, span], R1.at[span], c1_s.at[a], c1_r.at[a], sibling)
+                T1[h, 256 * m : 256 * m + 256, :] = out[:, 128 * h : 128 * h + 128]
+        span = pl.ds(256 * first_tap, 256 * (last_tap - first_tap))
+        return send(T1.at[other, span], R1.at[span], c1_s.at[n], c1_r.at[n], sibling)
+
+    def both_one(copies, first_tap, last_tap):
+        for copy in copies:
+            copy.wait_recv()
+
+        @pl.loop(first_tap, last_tap)
+        def _(g):
+            span = pl.ds(pl.multiple_of(256 * g, 256), 256)
+            S[2, span] = (T1[core, span].astype(f32) + R1[span].astype(f32)).astype(bf16)
 
     core_two = [two_taps(0, 3, 0), two_taps(3, 5, 1), two_taps(5, 7, 2), two_taps(7, 9, 3)]
+    B[15, 0:64] += dot_nt(C[8], tap(0, 1))
+    B[15, 64:128] += dot_nt(C[8], tap(0, 2)) + dot_nt(Cs[8], tap(0, 0))
+    for a in range(3):
+        fixes[a] = dot_nt(beside.astype(bf16), tap(a, 0))
+    for i in range(8):
+        B[2 * i, 127:128] += fixes[1, i : i + 1]
+        below = fixes[2, i : i + 1]
+        B[2 * i + 1, 127:128] += below + fixes[0, i + 1 : i + 2] if i < 7 else below
+
+    @pl.loop(0, 16)
+    def _(p):
+        V[p + 1, :, 256:512] = (B[p] * D[p]).astype(bf16)
+
+    for p in range(16):
+        edge32[0, p : p + 1] = V[p + 1, 0:16, 256:512].astype(f32)[0:1]
+        edge32[1, p : p + 1] = V[p + 1, 112:128, 256:512].astype(f32)[15:16]
+    pedges[...] = edge32[...].astype(bf16)
+    plast[0] = V[1, :, 256:512]
+    plast[1] = V[16, :, 256:512]
+    pg_halo = send_halos(plast.at[0], plast.at[1], pedges, prow, pcol, pg_s, pg_r)
+
     both_two(core_two[:2], 0, 5)
     g0 = [stage1(0), stage1(1)]
-    core_one = [one_taps(0)]
+    core_one = [one_taps(0, 2, 0)]
     both_two(core_two[2:], 5, 9)
     g1 = [stage1(2), stage1(3)]
-    core_one += [one_taps(1), one_taps(2)]
+    core_one += [one_taps(2, 5, 1), one_taps(5, 7, 2)]
+    both_one(core_one[:2], 0, 5)
+    g2 = [stage1(4), stage1(5)]
+    core_one += [one_taps(7, 9, 3)]
+    both_one(core_one[2:], 5, 9)
+    g3 = [stage1(6), stage1(7)]
 
     for copy in pg_halo:
         copy.wait_recv()
@@ -412,16 +447,6 @@
     for place, r, none in ((0, 0, row == 0), (1, 17, row == ROWS - 1)):
         values = jnp.where(none, 0.0, prow[place].astype(f32))
         shifted(V, r, values[0:64], values[64:128], left[r : r + 1], right[r : r + 1], True)
-
-    for copy in core_one:
-        copy.wait_recv()
-
-    @pl.loop(0, 9)
-    def _(g):
-        span = pl.ds(pl.multiple_of(256 * g, 256), 256)
-        S[2, span] = (T1[core, span].astype(f32) + R1[span].astype(f32)).astype(bf16)
-
-    g2 = [stage1(4), stage1(5)]
 
     def image_rows(g):
         terms = []
@@ -438,7 +463,7 @@
                 F[p, h, pl.ds(1, 64, stride=2), :] = acc[u, 64:128, 128 * h : 128 * h + 128]
             image_grad[p] = jnp.concatenate([F[p, 0], F[p, 1]], axis=1).astype(bf16)
 
-    pl.loop(0, 4)(image_rows)
+    pl.loop(0, 1)(image_rows)
 
     def pair(step, g, arrived):
         return [step(2 * g, arrived[0]), step(2 * g + 1, arrived[1])]
@@ -451,20 +476,27 @@
             copy.wait_recv()
 
     g0 = pair(stage2, 0, g0)
+    pl.loop(1, 3)(image_rows)
     g1 = pair(stage2, 1, g1)
     g0 = stage_z(0, both(g0))
     g2 = pair(stage2, 2, g2)
+    g3 = pair(stage2, 3, g3)
     g1 = stage_z(1, both(g1))
+    pl.loop(3, 4)(image_rows)
+    g2 = stage_z(2, both(g2))
+    g3 = stage_z(3, both(g3))
     g0 = gather_z(0, g0)
-    g2 = stage_z(2, both(g2))
     g1 = gather_z(1, g1)
+    g2 = gather_z(2, g2)
+    g3 = gather_z(3, g3)
     g0 = pair(gather2, 0, [g0, []])
-    g2 = gather_z(2, g2)
     g1 = pair(gather2, 1, [g1, []])
+    g2 = pair(gather2, 2, [g2, []])
+    g3 = pair(gather2, 3, [g3, []])
     g0 = pair(gather1, 0, g0)
-    g2 = pair(gather2, 2, [g2, []])
     g1 = pair(gather1, 1, g1)
     g2 = pair(gather1, 2, g2)
+    g3 = pair(gather1, 3, g3)
     g0 = pair(forward, 0, g0)
     g1 = pair(forward, 1, g1)
 
@@ -479,30 +511,39 @@
 
         return lax.fori_loop(0, 9, add, jnp.zeros((8, 128), f32))
 
+    g2 = pair(forward, 2, g2)
     arrive(g0)
     arrive(g1)
-    squares[0] = squares_of((0, 1))
-    g2 = pair(forward, 2, g2)
+    sum_two = jnp.sum(squares_of((0, 1)))
+    g3 = pair(forward, 3, g3)
+    scale_two = lax.rsqrt(sum_two / (9.0 * 256 * 512) + 1e-06)
+
+    @pl.loop(0, 9)
+    def _(g):
+        span = pl.ds(pl.multiple_of(256 * g, 256), 256)
+        for c in range(2):
+            for j in range(2):
+                two[span, 256 * c + 128 * j : 256 * c + 128 * j + 128] = (G[j, c, span].astype(f32) * scale_two).astype(bf16)
+
     arrive(g2)
-    squares[1] = squares_of((2,))
+    arrive(g3)
+    squares[...] = squares_of((2,))
 
     for copy in pending:
         copy.wait_send()
 
 
-def scaled(rows, G, squares, image_grad, two, one, two_v, one_v, sem):
-    copies = [pltpu.make_async_copy(rows, image_grad, sem.at[0])]
-    copies[0].start()
-    scale = [lax.rsqrt(jnp.sum(squares[n]) / count + 1e-06) for n, count in ((0, 9.0 * 256 * 512), (1, 9.0 * 256 * 256))]
+def written(rows, two_v, G, squares, image_grad, two, one, one_v, sem):
+    copies = [pltpu.make_async_copy(rows, image_grad, sem.at[0]), pltpu.make_async_copy(two_v, two, sem.at[1])]
+    for copy in copies:
+        copy.start()
+    scale = lax.rsqrt(jnp.sum(squares[...]) / (9.0 * 256 * 256) + 1e-06)
     for a in range(3):
         span = pl.ds(768 * a, 768)
         for c in range(2):
-            for j in range(2):
-                two_v[span, 256 * c + 128 * j : 256 * c + 128 * j + 128] = (G[j, c, span].astype(f32) * scale[0]).astype(bf16)
-            one_v[span, 128 * c : 128 * c + 128] = (G[2, c, span].astype(f32) * scale[1]).astype(bf16)
-        for n, (src, dst) in enumerate(((two_v, two), (one_v, one))):
-            copies.append(pltpu.make_async_copy(src.at[span], dst.at[span], sem.at[1 + 2 * a + n]))
-            copies[-1].start()
+            one_v[span, 128 * c : 128 * c + 128] = (G[2, c, span].astype(f32) * scale).astype(bf16)
+        copies.append(pltpu.make_async_copy(one_v.at[span], one.at[span], sem.at[2 + a]))
+        copies[-1].start()
     for copy in copies:
         copy.wait()
 
@@ -511,40 +552,40 @@
     vmem = pl.BlockSpec(memory_space=pltpu.VMEM)
     hbm = pl.BlockSpec(memory_space=pl.ANY)
     dma = pltpu.SemaphoreType.DMA
-    pairs = [(8,), (3,), (8,), (4,), (3,), (6, 3), (6, 3), (3, 7), (3, 7), (6, 3), (6, 3), (6, 4)]
+    pairs = [(8,), (3,), (8,), (4,), (4,), (8, 3), (8, 3), (4, 7), (4, 7), (8, 3), (8, 3), (8, 4)]
     scratch = [
         ((16, 128, 256), bf16), ((2304, 256), bf16), ((2304, 512), bf16), ((8, 64, 512), bf16),
         ((18, 2, 128, 128), f32), ((18, 128, 768), bf16), ((18, 128, 768), bf16),
         ((2, 2, 8, 64, 256), bf16), ((16, 128, 256), f32), ((16, 128, 256), f32), ((9, 64, 512), bf16), ((9, 64, 512), bf16),
         ((2, 16, 256), f32), ((2, 16, 256), bf16), ((2, 128, 256), bf16), ((2, 3, 16, 256), bf16),
         ((16, 512), bf16), ((64, 512), bf16), ((2, 16, 512), bf16),
-        ((2, 16, 256), bf16), ((2, 128, 256), bf16), ((2, 3, 16, 256), bf16),
+        ((2, 16, 256), bf16), ((2, 128, 256), bf16), ((2, 128, 256), bf16), ((2, 3, 16, 256), bf16),
         ((24, 256), f32), ((24, 256), f32), ((3, 16, 256), f32),
         ((2, 2304, 256), bf16), ((2304, 256), bf16), ((2, 2304, 128), bf16), ((2304, 128), bf16),
-        ((3, 2304, 128), bf16), ((3, 3, 576, 128), bf16), ((3, 576, 128), bf16), ((3, 3, 144, 128), bf16),
-        ((3, 8, 32, 128), bf16), ((3, 8, 32, 128), bf16),
+        ((3, 2304, 128), bf16), ((4, 3, 576, 128), bf16), ((4, 576, 128), bf16), ((4, 3, 144, 128), bf16),
+        ((4, 8, 32, 128), bf16), ((4, 8, 32, 128), bf16),
     ]
-    kept = [pltpu.VMEM((16, 128, 256), bf16), pltpu.VMEM((3, 2, 2304, 128), bf16), pltpu.VMEM((2, 8, 128), f32)]
-    rows, sums, squares = pl.pallas_call(
+    kept = [pltpu.VMEM(s, d) for s, d in (((16, 128, 256), bf16), ((2304, 512), bf16), ((3, 2, 2560, 128), bf16), ((8, 128), f32))]
+    kept_arrays = pl.pallas_call(
         kernel,
         out_shape=kept,
         in_specs=[hbm] * 4,
-        out_specs=[vmem] * 3,
+        out_specs=[vmem] * 4,
         scratch_shapes=[pltpu.VMEM(shape, kind) for shape, kind in scratch] + [dma((4,))] + [dma(s) for s in pairs for _ in range(2)],
         compiler_params=pltpu.CompilerParams(collective_id=0, has_side_effects=True, vmem_limit_bytes=50 << 20),
     )(image, kernel_one.reshape(2304, 256), kernel_two.reshape(2304, 512), cotangent)
     image_grad, two, one = pl.pallas_call(
-        scaled,
+        written,
         out_shape=(
             jax.ShapeDtypeStruct((16, 128, 256), bf16),
             jax.ShapeDtypeStruct((2304, 512), bf16),
             jax.ShapeDtypeStruct((2304, 256), bf16),
         ),
-        in_specs=[vmem] * 3,
+        in_specs=[vmem] * 4,
         out_specs=[hbm] * 3,
-        scratch_shapes=[pltpu.VMEM((2304, 512), bf16), pltpu.VMEM((2304, 256), bf16), dma((7,))],
+        scratch_shapes=[pltpu.VMEM((2304, 256), bf16), dma((5,))],
         compiler_params=pltpu.CompilerParams(vmem_limit_bytes=16 << 20),
-    )(rows, sums, squares)
+    )(*kept_arrays)
     return image_grad, one.reshape(kernel_one.shape), two.reshape(kernel_two.shape)
 
 

time: 70.3 us -> 68.1 us (0.969)
  Pallas kernels: 69.6 us -> 67.4 us
    pallas_call x1, Pallas kernels: 67.4 us -> 65.2 us  [on_device(): pl.pallas_call(kernel, out_shape=kept, in_specs=[hbm] * 4, out_specs=[vme...]
where the time goes in v3:
time: 68.1 us; the launch traced here: 68 us
  Pallas kernels  67.4 us (99%)
    pallas_call x1, Pallas kernels, on_device(): pl.pallas_call(kernel, out_shape=kept, in_specs=[hbm] * 4, out_specs=[vme...  65.2 us
    pallas_call x1, Pallas kernels, on_device(): pl.pallas_call(written, out_shape=(jax.ShapeDtypeStruct((16, 128, 256), b...  2.17 us

profile of v3, /device:TPU:1, one launch (start us, length us, event | category | flops | bytes accessed | tf_op | source)
XLA Modules:
  0.0 68.0 jit_solution(1623113355373419668)
XLA Ops:
  0.6 65.2 %shard_map.67 = (bf16[16,128,256]{2,1,0:T(8,128)(2,1)S(1)}, bf16[2304,512]{1,0:T(8,128)(2,1)S(1)}, bf16[3,2,2560,128]{3,2,1,0:T(8,128)(2,1)S(1)}, f32[8,128]{1,0:T(8,128)S(1)}) custom-call(bf16[16,128,256]{2,1,0:T(8,128)(2,1)} %image_hbm.1, bf16[2304,256]{1,0:T(8,128)(2,1)} %bitcast.5, bf16[2304,512]{1,0:T(8,128)(2,1)} %bitcast.4, bf16[8,64,512]{2,1,0:T(8,128)(2,1)} %cot_hbm.1), custom_call_target="tpu_custom_call" | custom-call | tf_op jit(solution)/shard_map/pallas_call | solution.py:569
  65.9 2.2 %shard_map.68 = (bf16[16,128,256]{2,1,0:T(8,128)(2,1)}, bf16[2304,512]{1,0:T(8,128)(2,1)}, bf16[2304,256]{1,0:T(8,128)(2,1)}) custom-call(bf16[16,128,256]{2,1,0:T(8,128)(2,1)S(1)} %get-tuple-element.10.rows, bf16[2304,512]{1,0:T(8,128)(2,1)S(1)} %get-tuple-element.11.two_v, bf16[3,2,2560,128]{3,2,1,0:T(8,128)(2,1)S(1)} %get-tuple-element.12.G, ...), custom_call_target="tpu_custom_call" | custom-call | tf_op jit(solution)/shard_map/pallas_call | solution.py:577

commit v4 on v3

--- a/solution.py
+++ b/solution.py
@@ -433,21 +433,6 @@
     both_one(core_one[2:], 5, 9)
     g3 = [stage1(6), stage1(7)]
 
-    for copy in pg_halo:
-        copy.wait_recv()
-    sides_of(pcol)
-
-    @pl.loop(0, 16)
-    def _(p):
-        shifted(
-            V, p + 1, V[p + 1, 0:64, 256:512].astype(f32), V[p + 1, 64:128, 256:512].astype(f32),
-            left[pl.ds(p + 1, 1)], right[pl.ds(p + 1, 1)], False,
-        )
-
-    for place, r, none in ((0, 0, row == 0), (1, 17, row == ROWS - 1)):
-        values = jnp.where(none, 0.0, prow[place].astype(f32))
-        shifted(V, r, values[0:64], values[64:128], left[r : r + 1], right[r : r + 1], True)
-
     def image_rows(g):
         terms = []
         for a in range(3):
@@ -463,7 +448,6 @@
                 F[p, h, pl.ds(1, 64, stride=2), :] = acc[u, 64:128, 128 * h : 128 * h + 128]
             image_grad[p] = jnp.concatenate([F[p, 0], F[p, 1]], axis=1).astype(bf16)
 
-    pl.loop(0, 1)(image_rows)
 
     def pair(step, g, arrived):
         return [step(2 * g, arrived[0]), step(2 * g + 1, arrived[1])]
@@ -476,15 +460,32 @@
             copy.wait_recv()
 
     g0 = pair(stage2, 0, g0)
-    pl.loop(1, 3)(image_rows)
+
+    for copy in pg_halo:
+        copy.wait_recv()
+    sides_of(pcol)
+
+    @pl.loop(0, 16)
+    def _(p):
+        shifted(
+            V, p + 1, V[p + 1, 0:64, 256:512].astype(f32), V[p + 1, 64:128, 256:512].astype(f32),
+            left[pl.ds(p + 1, 1)], right[pl.ds(p + 1, 1)], False,
+        )
+
+    for place, r, none in ((0, 0, row == 0), (1, 17, row == ROWS - 1)):
+        values = jnp.where(none, 0.0, prow[place].astype(f32))
+        shifted(V, r, values[0:64], values[64:128], left[r : r + 1], right[r : r + 1], True)
+
+    pl.loop(0, 2)(image_rows)
     g1 = pair(stage2, 1, g1)
     g0 = stage_z(0, both(g0))
     g2 = pair(stage2, 2, g2)
     g3 = pair(stage2, 3, g3)
     g1 = stage_z(1, both(g1))
-    pl.loop(3, 4)(image_rows)
+    pl.loop(2, 3)(image_rows)
     g2 = stage_z(2, both(g2))
     g3 = stage_z(3, both(g3))
+    pl.loop(3, 4)(image_rows)
     g0 = gather_z(0, g0)
     g1 = gather_z(1, g1)
     g2 = gather_z(2, g2)

time: 68.1 us -> 68.7 us (level)
  no operation moved by 1% of the time
where the time goes in v4:
time: 68.7 us; the launch traced here: 68.6 us
  Pallas kernels  68 us (99%)
    pallas_call x1, Pallas kernels, on_device(): pl.pallas_call(kernel, out_shape=kept, in_specs=[hbm] * 4, out_specs=[vme...  65.8 us
    pallas_call x1, Pallas kernels, on_device(): pl.pallas_call(written, out_shape=(jax.ShapeDtypeStruct((16, 128, 256), b...  2.17 us

profile of v4, /device:TPU:1, one launch (start us, length us, event | category | flops | bytes accessed | tf_op | source)
XLA Modules:
  0.0 68.6 jit_solution(10897027286590517047)
XLA Ops:
  0.6 65.8 %shard_map.67 = (bf16[16,128,256]{2,1,0:T(8,128)(2,1)S(1)}, bf16[2304,512]{1,0:T(8,128)(2,1)S(1)}, bf16[3,2,2560,128]{3,2,1,0:T(8,128)(2,1)S(1)}, f32[8,128]{1,0:T(8,128)S(1)}) custom-call(bf16[16,128,256]{2,1,0:T(8,128)(2,1)} %image_hbm.1, bf16[2304,256]{1,0:T(8,128)(2,1)} %bitcast.5, bf16[2304,512]{1,0:T(8,128)(2,1)} %bitcast.4, bf16[8,64,512]{2,1,0:T(8,128)(2,1)} %cot_hbm.1), custom_call_target="tpu_custom_call" | custom-call | tf_op jit(solution)/shard_map/pallas_call | solution.py:570
  66.5 2.2 %shard_map.68 = (bf16[16,128,256]{2,1,0:T(8,128)(2,1)}, bf16[2304,512]{1,0:T(8,128)(2,1)}, bf16[2304,256]{1,0:T(8,128)(2,1)}) custom-call(bf16[16,128,256]{2,1,0:T(8,128)(2,1)S(1)} %get-tuple-element.10.rows, bf16[2304,512]{1,0:T(8,128)(2,1)S(1)} %get-tuple-element.11.two_v, bf16[3,2,2560,128]{3,2,1,0:T(8,128)(2,1)S(1)} %get-tuple-element.12.G, ...), custom_call_target="tpu_custom_call" | custom-call | tf_op jit(solution)/shard_map/pallas_call | solution.py:578
